TPU v7x, 256 devices: a whole 4x4x8 slice. The times are simulated.
256 devices in a mesh: grp: 8 (over z), mp: 32 (over x, y, core).
Axes of the slice: x: 4, y: 4, z: 8, core: 2. Of those that a mesh axis runs over, the one named last changes fastest.
Arguments:
- activations: bfloat16 [16, 96, 8192], P('grp', None, 'mp'), may hold values from -6 to 6
- out_grads: bfloat16 [16, 96, 14336], P('grp', None, 'mp'), may hold values from -6 to 6
- valid_counts: int32 [16], P('grp'), may hold values from 24 to 96, as said below
- basis_in: bfloat16 [8192, 8192], P(None, 'mp'), may hold values from -0.0625 to 0.0625
- basis_out: bfloat16 [14336, 14336], P('grp', 'mp'), may hold values from -0.046875 to 0.046875
- eigvals: bfloat16 [14336, 8192], P('mp'), may hold values from 0.3 to 900
- query_out: bfloat16 [8, 16, 14336], P('grp', None, 'mp'), may hold values from -0.01171875 to 0.01171875
- query_in: bfloat16 [8, 16, 8192], P('grp', None, 'mp'), may hold values from -0.0625 to 0.0625
Outputs:
- scores: float32 [16, 8], P('grp')
Inputs may be any that keep to these rules, and one draw needn't show every extreme that they name: `valid_counts`: each count is at least a quarter of 96; in every draw some sequence has all 96 slots valid.
All inputs are finite; a program needn't handle non-finite values.
Results may differ from a plain program's by a relative error of at most 0.005.
Values may be sent and summed in bfloat16 or wider, within the bound.
A program may use at most 128 MiB of HBM per device.

v0:
```python
import jax
import jax.numpy as jnp
from jax import lax
from jax.sharding import PartitionSpec as P


def per_device(
    activations, out_grads, valid_counts, basis_in, basis_out, eigvals, query_out, query_in
):
    seq_count, length, feature_part = activations.shape
    query_count, factor_rank, hidden_part = query_out.shape
    token_rows = seq_count * length
    spectrum_sum = lax.psum(jnp.sum(eigvals.astype(jnp.float32)), "mp")
    hidden_all = hidden_part * lax.axis_size("mp")
    feature_all = feature_part * lax.axis_size("mp")
    damping = 0.1 * spectrum_sum / (hidden_all * feature_all)
    grads_full, qout_full = (
        lax.all_gather(out_grads, "mp", axis=2, tiled=True),
        lax.all_gather(query_out, "mp", axis=2, tiled=True),
    )
    acts_full, qin_full = (
        lax.all_gather(activations, "mp", axis=2, tiled=True),
        lax.all_gather(query_in, "mp", axis=2, tiled=True),
    )
    hidden_rows = jnp.concatenate(
        [
            grads_full.reshape(token_rows, hidden_all),
            qout_full.reshape(query_count * factor_rank, hidden_all),
        ],
        0,
    )
    feature_rows = jnp.concatenate(
        [
            acts_full.reshape(token_rows, feature_all),
            qin_full.reshape(query_count * factor_rank, feature_all),
        ],
        0,
    )
    rotated_in = jnp.dot(feature_rows, basis_in, preferred_element_type=jnp.float32).astype(
        jnp.bfloat16
    )
    rotated_out = jnp.dot(
        hidden_rows,
        lax.all_gather(basis_out, "grp", axis=0, tiled=True),
        preferred_element_type=jnp.float32,
    )
    rotated_out = rotated_out.astype(jnp.bfloat16)
    positions = lax.broadcasted_iota(jnp.int32, (seq_count, length), 1)
    keep_mask = (positions < valid_counts[:, None]).astype(jnp.bfloat16).reshape(token_rows, 1)
    kept_rows = jnp.concatenate([rotated_in[:token_rows] * keep_mask, rotated_in[token_rows:]], 0)
    wide_rows = lax.all_gather(kept_rows, "mp", axis=1, tiled=True)
    act_kept = wide_rows[:token_rows].reshape(seq_count, length, feature_all)
    qin_mine = wide_rows[token_rows:].reshape(query_count, factor_rank, feature_all)
    grad_rot = rotated_out[:token_rows].reshape(seq_count, length, hidden_part)
    qout_mine = rotated_out[token_rows:].reshape(query_count, factor_rank, hidden_part)
    qin_every, qout_every = (
        lax.all_gather(qin_mine, "grp", axis=0, tiled=True),
        lax.all_gather(qout_mine, "grp", axis=0, tiled=True),
    )
    query_total = qin_every.shape[0]
    qin_flat = qin_every.reshape(query_total * factor_rank, feature_all)
    qout_wide = qout_every.reshape(query_total * factor_rank, hidden_part).astype(jnp.float32)
    denominator = eigvals.astype(jnp.float32) + damping
    partials = []
    for sequence in range(seq_count):
        outer_sum = lax.dot_general(
            grad_rot[sequence],
            act_kept[sequence],
            (((0,), (0,)), ((), ())),
            preferred_element_type=jnp.float32,
        )
        weighted = (outer_sum / denominator).astype(jnp.bfloat16)
        mixed_rows = lax.dot_general(
            weighted, qin_flat, (((1,), (1,)), ((), ())), preferred_element_type=jnp.float32
        )
        summed = jnp.sum(qout_wide.T * mixed_rows, axis=0)
        partials.append(jnp.sum(summed.reshape(query_total, factor_rank), axis=1))
    partial_scores = jnp.stack(partials, 0)
    return lax.psum(partial_scores, "mp")


def solution(mesh):
    in_specs = (
        P("grp", None, "mp"),
        P("grp", None, "mp"),
        P("grp"),
        P(None, "mp"),
        P("grp", "mp"),
        P("mp", None),
        P("grp", None, "mp"),
        P("grp", None, "mp"),
    )
    out_specs = P("grp", None)
    return jax.shard_map(
        per_device, mesh=mesh, in_specs=in_specs, out_specs=out_specs, check_vma=False
    )
```

profile of v0, /device:TPU:1, one launch (start us, length us, event | category | flops | bytes accessed | tf_op | source)
XLA Modules:
  0.0 446.3 jit_solution(3785352018932103756)
XLA Ops:
  6.5 0.0 all-gather.12.cloned.1.call-start
  6.5 0.7 all-gather.12.cloned.1.call-update
  7.3 0.0 all-gather.14.cloned.1.call-start
  7.3 0.7 compare_convert_fusion
  8.0 0.1 reshape.68
  8.1 26.4 %all_gather.29 = bf16[1,16,8192]{2,1,0:T(8,128)(2,1)S(1)} all-gather(bf16[1,16,256]{2,1,0:T(8,128)(2,1)} %param.15), channel_id=1, replica_groups=mesh['grp'=8,'mp'=32] {'mp'}, dimensions={2}, use_global_device_ids=true | all-gather | bytes 270336 | tf_op jit(solution)/shard_map/all_gather | solution.py:23
  34.5 31.5 %all-gather.12.cloned.1.call-done = bf16[2,96,8192]{2,1,0:T(8,128)(2,1)} async-done(((bf16[2,96,256]{2,1,0:T(8,128)(2,1)}), bf16[2,96,8192]{2,1,0:T(8,128)(2,1)}) %all-gather.12.cloned.1.call-update) | async-done | bytes 3145744 | tf_op jit(solution)/shard_map/all_gather | solution.py:22
  66.0 0.0 copy-start
  66.0 4.2 fusion.27
  70.3 0.0 copy-start.1
  70.3 0.1 slice_multiply_fusion
  70.4 0.7 pad_maximum_fusion
  71.0 0.0 all-gather.14.cloned.1.call-update
  71.1 0.0 all-gather.8.cloned.1.call-start
  71.1 0.0 copy-done
  71.1 0.9 copy.15
  72.0 0.0 all-gather.8.cloned.1.call-update
  72.0 0.0 all-gather.10.cloned.1.call-start
  72.1 0.5 all-gather.10.cloned.1.call-update
  72.6 0.0 all-gather.16.cloned.1.call-start
  72.6 50.5 %all-gather.14.cloned.1.call-done = bf16[208,8192]{1,0:T(8,128)(2,1)} async-done(((bf16[208,256]{1,0:T(8,128)(2,1)}), bf16[208,8192]{1,0:T(8,128)(2,1)}) %all-gather.14.cloned.1.call-update) | async-done | bytes 3407888 | tf_op jit(solution)/shard_map/all_gather | solution.py:51
  123.2 1.7 slice.47
  124.8 0.0 all-gather.16.cloned.1.call-update
  124.9 7.5 %convert_reduce_fusion = f32[]{:T(128)} fusion(bf16[448,8192]{1,0:T(8,128)(2,1)} %param.13), kind=kLoop, calls=%fused_computation.1 | loop fusion | flops 7340031 | bytes 7340036 | tf_op jit(solution)/shard_map/reduce_sum | solution.py:13
  132.3 63.4 %psum.14 = f32[]{:T(128)} all-reduce(f32[]{:T(128)} %convert_reduce_fusion), channel_id=1, replica_groups=mesh['grp'=8,'mp'=32] {'mp'}, use_global_device_ids=true, to_apply=%region_1.0 | all-reduce | flops 1 | bytes 8 | tf_op jit(solution)/shard_map/psum | solution.py:13
  195.7 0.0 copy-done.1
  195.7 0.2 copy.17
  195.9 35.3 %all_gather.25 = bf16[1,16,14336]{1,0,2:T(2,128)(2,1)} all-gather(bf16[1,16,448]{1,0,2:T(2,128)(2,1)S(1)} %copy.17), channel_id=1, replica_groups=mesh['grp'=8,'mp'=32] {'mp'}, dimensions={2}, use_global_device_ids=true | all-gather | bytes 473088 | tf_op jit(solution)/shard_map/all_gather | solution.py:19
  231.2 13.5 %copy.18 = bf16[1,16,14336]{2,1,0:T(8,128)(2,1)S(1)} copy(bf16[1,16,14336]{1,0,2:T(2,128)(2,1)} %all_gather.25) | data formatting | bytes 917504 | tf_op jit(solution)/shard_map/all_gather | solution.py:19
  245.4 0.0 all-gather.8.cloned.1.call-done
  245.4 16.0 %copy.16 = bf16[2,96,14336]{2,1,0:T(8,128)(2,1)} copy(bf16[2,96,14336]{1,0,2:T(2,128)(2,1)} %all-gather.8.cloned.1.call-done) | data formatting | bytes 11010048 | tf_op jit(solution)/shard_map/all_gather | solution.py:18
  261.4 56.5 %all-gather.10.cloned.1.call-done = bf16[14336,448]{0,1:T(8,128)(2,1)} async-done(((bf16[1792,448]{0,1:T(8,128)(2,1)}), bf16[14336,448]{0,1:T(8,128)(2,1)}) %all-gather.10.cloned.1.call-update) | async-done | bytes 12845072 | tf_op jit(solution)/shard_map/all_gather | solution.py:44
  317.9 10.0 %fusion.18 = bf16[208,448]{1,0:T(8,128)(2,1)S(1)} fusion(bf16[14336,448]{0,1:T(8,128)(2,1)} %all-gather.10.cloned.1.call-done, bf16[16,14336]{1,0:T(8,128)(2,1)S(1)} %bitcast.14, bf16[192,14336]{1,0:T(8,128)(2,1)} %bitcast.13), kind=kOutput, calls=%fused_computation.18 | convolution fusion | flops 2683792384 | bytes 18995200 | tf_op jit(solution)/shard_map/dot_general | solution.py:42
  327.9 19.6 %all-gather = bf16[128,448]{1,0:T(8,128)(2,1)S(1)} all-gather(bf16[16,448]{1,0:T(8,128)(2,1)S(1)} %slice.42), channel_id=2, replica_groups=mesh['grp'=8,'mp'=32] {'grp'}, dimensions={0}, use_global_device_ids=true | all-gather | bytes 129024 | tf_op jit(solution)/shard_map/all_gather | solution.py:58
  347.5 8.8 %all-gather.16.cloned.1.call-done = bf16[128,8192]{1,0:T(8,128)(2,1)} async-done(((bf16[16,8192]{1,0:T(8,128)(2,1)}), bf16[128,8192]{1,0:T(8,128)(2,1)}) %all-gather.16.cloned.1.call-update) | async-done | bytes 2097168 | tf_op jit(solution)/shard_map/all_gather | solution.py:57
  356.3 0.0 copy-start.2
  356.3 8.7 %fusion.33 = f32[128]{0:T(128)S(1)} fusion(bf16[128,8192]{1,0:T(8,128)(2,1)} %all-gather.16.cloned.1.call-done, bf16[448,8192]{1,0:T(8,128)(2,1)} %param.13, f32[]{:T(128)S(6)} %div.9, bf16[208,8192]{1,0:T(8,128)(2,1)} %all-gather.14.cloned.1.call-done, bf16[128,448]{1,0:T(8,128)(2,1)S(1)} %all-gather, bf16[208,448]{1,0:T(8,128)(2,1)S(1)} %fusion.18), kind=kOutput, calls=%fused_computation.23 | convolution fusion | flops 1659019136 | bytes 11239940 | tf_op jit(solution)/shard_map/dot_general | solution.py:73
  364.9 0.1 reshape.66
  365.0 0.0 copy-done.2
  365.0 8.0 %fusion.30 = f32[128]{0:T(128)S(1)} fusion(bf16[128,8192]{1,0:T(8,128)(2,1)S(1)} %copy-done.2, bf16[448,8192]{1,0:T(8,128)(2,1)} %param.13, f32[]{:T(128)S(6)} %div.9, bf16[208,8192]{1,0:T(8,128)(2,1)} %all-gather.14.cloned.1.call-done, bf16[128,448]{1,0:T(8,128)(2,1)S(1)} %all-gather, bf16[208,448]{1,0:T(8,128)(2,1)S(1)} %fusion.18), kind=kOutput, calls=%fused_computation.22 | convolution fusion | flops 1659019136 | bytes 11239940 | tf_op jit(solution)/shard_map/dot_general | solution.py:73
  373.0 0.1 reshape.67
  373.1 0.1 reduce_sum.47
  373.2 0.1 reduce_sum.49
  373.4 66.4 %psum.15 = f32[2,8]{1,0:T(2,128)} all-reduce(f32[2,8]{1,0:T(2,128)S(1)} %pad_maximum_fusion.1), channel_id=1, replica_groups=mesh['grp'=8,'mp'=32] {'mp'}, use_global_device_ids=true, to_apply=%region_6.0 | all-reduce | flops 16 | bytes 128 | tf_op jit(solution)/shard_map/psum | solution.py:79
  (3 shorter events, 0.0 us)
Async XLA Ops:
  6.5 59.5 %all-gather.12.cloned.1.call-start = ((), (), s32[]{:S(2)}) async-start(), calls=%async_computation.2 | async-start | bytes 3244032 | tf_op jit(solution)/shard_map/all_gather | solution.py:22
  7.3 115.9 %all-gather.14.cloned.1.call-start = ((), (), s32[]{:S(2)}) async-start(), calls=%async_computation.3 | async-start | bytes 3514368 | tf_op jit(solution)/shard_map/all_gather | solution.py:51
  66.0 5.1 %copy-start = (bf16[2,96,448]{2,1,0:T(8,128)(2,1)S(1)}, bf16[2,96,448]{2,1,0:T(8,128)(2,1)}, u32[]{:S(2)}) copy-start(bf16[2,96,448]{2,1,0:T(8,128)(2,1)} %param.9) | copy-start | bytes 516100
  70.3 125.4 %copy-start.1 = (bf16[1,16,448]{2,1,0:T(8,128)(2,1)S(1)}, bf16[1,16,448]{2,1,0:T(8,128)(2,1)}, u32[]{:S(2)}) copy-start(bf16[1,16,448]{2,1,0:T(8,128)(2,1)} %param.14) | copy-start | bytes 43012
  71.1 174.3 %all-gather.8.cloned.1.call-start = ((), (), s32[]{:S(2)}) async-start(), calls=%async_computation | async-start | bytes 7569408 | tf_op jit(solution)/shard_map/all_gather | solution.py:18
  72.0 245.9 %all-gather.10.cloned.1.call-start = ((), (), s32[]{:S(2)}) async-start(), calls=%async_computation.1 | async-start | bytes 14450688 | tf_op jit(solution)/shard_map/all_gather | solution.py:44
  72.6 283.7 %all-gather.16.cloned.1.call-start = ((), (), s32[]{:S(2)}) async-start(), calls=%async_computation.4 | async-start | bytes 2359296 | tf_op jit(solution)/shard_map/all_gather | solution.py:57
  356.3 8.7 %copy-start.2 = (bf16[128,8192]{1,0:T(8,128)(2,1)S(1)}, bf16[128,8192]{1,0:T(8,128)(2,1)}, u32[]{:S(2)}) copy-start(bf16[128,8192]{1,0:T(8,128)(2,1)} %all-gather.16.cloned.1.call-done) | copy-start | bytes 6291460
Sparse Core Ops, SparseCore 0:
  9.8 56.1 all-gather.11
  71.2 51.9 all-gather.13
  125.7 55.5 all-gather.7
  183.0 134.8 all-gather.9
  319.5 36.7 all-gather.15
where the time goes:
time: 447 us; the launch traced here: 446 us
  blocking collectives  211 us (47%)
  waiting for transfers between devices  149 us (33%)
  local copies, waits for them, and re-layouts  32.5 us (7%)
  matrix products  30.8 us (7%)
  between operations  13.9 us (3%)
  other arithmetic  9.19 us (2%)
    psum x1, blocking collectives, per_device(): return lax.psum(partial_scores, 'mp')  66.4 us
    psum x1, blocking collectives, per_device(): spectrum_sum = lax.psum(jnp.sum(eigvals.astype(jnp.float32)), 'mp')  63.4 us
    all_gather x1, waiting for transfers between devices, per_device(): lax.all_gather(basis_out, 'grp', axis=0, tiled=True)  56.5 us
    all_gather x1, waiting for transfers between devices, per_device(): wide_rows = lax.all_gather(kept_rows, 'mp', axis=1, tiled=True)  50.5 us
    all_gather x1, blocking collectives, per_device(): lax.all_gather(query_out, 'mp', axis=2, tiled=True)  35.3 us
    all_gather x1, waiting for transfers between devices, per_device(): lax.all_gather(activations, 'mp', axis=2, tiled=True)  31.5 us
    all_gather x1, blocking collectives, per_device(): lax.all_gather(query_in, 'mp', axis=2, tiled=True)  26.4 us
    all_gather x1, blocking collectives, per_device(): lax.all_gather(qout_mine, 'grp', axis=0, tiled=True)  19.6 us
  transfers between devices with their start and end apart: 5, of which 4 were waited for; matrix products, arithmetic and copies ran while one was open for 11% of the time, Pallas kernels for 0%

commit v1 on v0

v1 whole, which is shorter than its diff:
```python
import functools

import jax
import jax.numpy as jnp
from jax import lax
from jax.experimental import pallas as pl
from jax.experimental.pallas import tpu as pltpu
from jax.sharding import PartitionSpec as P

MESH = pl.DeviceIdType.MESH
F32 = jnp.float32
BF16 = jnp.bfloat16

SIDE = 4
PLANES = 8
DEVICES = 32
TOKENS = 192
RANK = 16
ROWS = TOKENS + RANK
LEN = 96
HID = 448
FEAT = 256
QROWS = PLANES * RANK
WIDE = TOKENS + QROWS
FF = HID * DEVICES
D = FEAT * DEVICES


def mod(value, n):
    return lax.rem(value + 2 * n, n)


class Gather:
    def __init__(self, place, buf, send_sems, recv_sems):
        self.z, self.m, self.x, self.y, self.core = place
        self.buf, self.send_sems, self.recv_sems = buf, send_sems, recv_sems
        self.p1 = self.x * (1 - self.core) + self.y * self.core
        self.p2 = self.y * (1 - self.core) + self.x * self.core
        self.sibling = self.m + 1 - 2 * self.core
        self.sent = []

    def slot(self, d1, d2):
        a, b = mod(self.p1 + d1, SIDE), mod(self.p2 + d2, SIDE)
        x = a * (1 - self.core) + b * self.core
        y = b * (1 - self.core) + a * self.core
        return (x * SIDE + y) * 2 + self.core

    def copy(self, slot, to, index):
        return pltpu.make_async_remote_copy(
            src_ref=self.buf.at[slot],
            dst_ref=self.buf.at[slot],
            send_sem=self.send_sems.at[index],
            recv_sem=self.recv_sems.at[slot],
            device_id=(self.z, to),
            device_id_type=MESH,
        )

    def send(self, slot, to):
        copy = self.copy(slot, to, len(self.sent))
        copy.start()
        self.sent.append(copy)

    def arrive(self, slot):
        self.copy(slot, self.sibling, 0).wait_recv()

    def event(self, offset, first=(), second=()):
        slot = self.slot(*offset)
        if offset != (0, 0):
            self.arrive(slot)
        for step in first:
            self.send(slot, self.slot(step, 0))
        for step in second:
            self.send(slot, self.slot(0, step))
        self.send(slot, self.sibling)

    def events(self):
        both = (1, -1)
        plan = [
            ((0, 0), both, both),
            ((-1, 0), (1,), both),
            ((1, 0), (), both),
            ((0, -1), (), (1,)),
            ((0, 1), (), ()),
            ((2, 0), (), both),
            ((-1, -1), (), ()),
            ((-1, 1), (), (-1,)),
            ((1, -1), (), ()),
            ((1, 1), (), (-1,)),
            ((2, -1), (), (1,)),
            ((2, 1), (), ()),
            ((0, 2), (), ()),
            ((-1, 2), (), ()),
            ((1, 2), (), ()),
            ((2, 2), (), ()),
        ]
        return [functools.partial(self.event, *entry) for entry in plan]

    def rest(self):
        def body(chip, carry):
            self.arrive(chip * 2 + 1 - self.core)
            return carry

        lax.fori_loop(0, SIDE * SIDE, body, 0)

    def finish(self):
        for copy in self.sent:
            copy.wait_send()


def plane_sum(place, tiles, landed, send_sems, recv_sems):
    z, m, x, y, core = place
    sent = []

    def exchange(stage, base, peers):
        for index, peer in enumerate(peers):
            copy = pltpu.make_async_remote_copy(
                src_ref=tiles.at[stage],
                dst_ref=landed.at[base + index],
                send_sem=send_sems.at[base + index],
                recv_sem=recv_sems.at[base + index],
                device_id=(z, peer),
                device_id_type=MESH,
            )
            copy.start()
            sent.append(copy)
        total = tiles[stage]
        for index in range(len(peers)):
            sent[base + index].wait_recv()
            total = total + landed[base + index]
        return total

    total = exchange(0, 0, [m + 1 - 2 * core])
    tiles[1] = total
    total = exchange(1, 1, [(mod(x + o, SIDE) * SIDE + y) * 2 + core for o in (1, 2, 3)])
    tiles[2] = total
    total = exchange(2, 4, [(x * SIDE + mod(y + o, SIDE)) * 2 + core for o in (1, 2, 3)])
    return total, sent


def kernel(
    acts,
    grads,
    counts,
    basis_in,
    basis_out,
    eigvals,
    query_out,
    query_in,
    out,
    bin_v,
    bout_v,
    eig_v,
    acts_all,
    stage,
    grads_all,
    wide_all,
    acc_in,
    send_a,
    send_b,
    got_a,
    got_b,
    qout_all,
    pad,
    left,
    qout_t,
    mixed,
    tiles1,
    landed1,
    tiles2,
    landed2,
    local_sems,
    acts_send,
    acts_recv,
    grads_send,
    grads_recv,
    wide_send,
    wide_recv,
    perm_sems,
    qin_send,
    qin_recv,
    qout_send,
    qout_recv,
    a_send,
    a_recv,
    b_send,
    b_recv,
    sum1_send,
    sum1_recv,
    sum2_send,
    sum2_recv,
):
    z = lax.axis_index("grp")
    m = lax.axis_index("mp")
    core = lax.rem(m, 2)
    chip = lax.div(m, 2)
    x, y = lax.div(chip, SIDE), lax.rem(chip, SIDE)
    place = (z, m, x, y, core)

    loads = []

    def load(src, dst):
        copy = pltpu.make_async_copy(src, dst, local_sems.at[len(loads)])
        copy.start()
        loads.append(copy)

    load(acts.at[0], acts_all.at[m, pl.ds(0, LEN)])
    load(acts.at[1], acts_all.at[m, pl.ds(LEN, LEN)])
    load(query_in.at[0], acts_all.at[m, pl.ds(TOKENS, RANK)])
    load(grads.at[0], stage.at[pl.ds(0, LEN)])
    load(grads.at[1], stage.at[pl.ds(LEN, LEN)])
    load(query_out.at[0], stage.at[pl.ds(TOKENS, RANK)])
    load(eigvals, eig_v)
    load(basis_in, bin_v)
    load(basis_out, bout_v)

    plane = lax.div(m, 4)
    y_low, y_high = lax.rem(y, 2), lax.div(y, 2)

    def device_of(target, j_high, j_low, source):
        ring = mod(target - source - 4 * j_low, PLANES)
        high = lax.rem(ring, 2)
        low = lax.rem(j_high + lax.rem(target, 2) + high, 2)
        return (lax.div(ring, 2) * SIDE + 2 * high + low) * 2 + j_low

    to = device_of(plane, y_low, core, z)
    from_plane = mod(z - (2 * x + y_high) - 4 * core, PLANES)
    from_device = 4 * z + 2 * lax.rem(y_low + y_high + lax.rem(z, 2), 2) + core
    stays = jnp.logical_and(plane == z, to == m)

    barrier = pltpu.get_barrier_semaphore()
    flat = [(mod(x + o, SIDE) * SIDE + y) * 2 + core for o in (1, 2, 3)]
    flat += [(x * SIDE + mod(y + o, SIDE)) * 2 + core for o in (1, 2, 3)]
    flat.append(m + 1 - 2 * core)
    for peer in flat:
        pl.semaphore_signal(barrier, inc=1, device_id=(z, peer), device_id_type=MESH)
    for o in range(1, PLANES):
        pl.semaphore_signal(
            barrier, inc=1, device_id=(mod(z + o, PLANES), m), device_id_type=MESH
        )

    @pl.when(jnp.logical_not(stays))
    def _():
        pl.semaphore_signal(
            barrier, inc=1, device_id=(from_plane, from_device), device_id_type=MESH
        )

    moves = jnp.where(stays, 0, 1)
    pl.semaphore_wait(barrier, len(flat) + PLANES - 1 + moves)

    permute = pltpu.make_async_remote_copy(
        src_ref=stage,
        dst_ref=grads_all.at[to],
        send_sem=perm_sems.at[0],
        recv_sem=perm_sems.at[1],
        device_id=(plane, to),
        device_id_type=MESH,
    )
    keep = pltpu.make_async_copy(stage, grads_all.at[m], perm_sems.at[2])

    for copy in loads[:3]:
        copy.wait()
    gather_acts = Gather(place, acts_all, acts_send, acts_recv)
    acts_events = gather_acts.events()
    acts_events[0]()
    for copy in loads[3:6]:
        copy.wait()

    @pl.when(stays)
    def _():
        keep.start()

    @pl.when(jnp.logical_not(stays))
    def _():
        permute.start()

    for event in acts_events[1:6]:
        event()

    loads[6].wait()

    def add_eig(slot, total):
        columns = pl.ds(pl.multiple_of(slot * FEAT, FEAT), FEAT)
        block = eig_v[:, columns].astype(F32).reshape(HID // 8, 8, FEAT)
        return total + jnp.sum(block, axis=0)

    eig_sum = lax.fori_loop(0, DEVICES, add_eig, jnp.zeros((8, FEAT), F32))
    tiles1[0] = eig_sum[:, :128] + eig_sum[:, 128:]

    for event in acts_events[6:]:
        event()

    @pl.when(stays)
    def _():
        keep.wait()

    @pl.when(jnp.logical_not(stays))
    def _():
        permute.wait()

    gather_grads = Gather(place, grads_all, grads_send, grads_recv)
    grads_events = gather_grads.events()
    grads_events[0]()

    gather_acts.rest()
    loads[7].wait()
    acc_in[...] = jnp.zeros_like(acc_in)

    def rotate_in(slot, carry):
        rows = pl.ds(pl.multiple_of(slot * FEAT, FEAT), FEAT)
        acc_in[...] += jnp.dot(acts_all[slot], bin_v[rows, :], preferred_element_type=F32)
        return carry

    lax.fori_loop(0, DEVICES, rotate_in, 0)
    position = lax.broadcasted_iota(jnp.int32, (LEN, FEAT), 0)
    for s in range(2):
        rows = pl.ds(s * LEN, LEN)
        kept = jnp.where(position < counts[s], acc_in[rows, :], 0.0)
        wide_all[m, rows, :] = kept.astype(BF16)
    my_query = pl.ds(pl.multiple_of(TOKENS + z * RANK, RANK), RANK)
    wide_all[m, my_query, :] = acc_in[pl.ds(TOKENS, RANK), :].astype(BF16)
    qin_sent = []
    for o in range(1, PLANES):
        copy = pltpu.make_async_remote_copy(
            src_ref=wide_all.at[m, my_query],
            dst_ref=wide_all.at[m, my_query],
            send_sem=qin_send.at[o],
            recv_sem=qin_recv.at[o],
            device_id=(mod(z + o, PLANES), m),
            device_id_type=MESH,
        )
        copy.start()
        qin_sent.append(copy)

    for event in grads_events[1:6]:
        event()
    eig_total, sum1_sent = plane_sum(place, tiles1, landed1, sum1_send, sum1_recv)
    damping = 0.1 * jnp.sum(eig_total) / (FF * D)
    for event in grads_events[6:]:
        event()

    for copy in qin_sent:
        copy.wait_recv()
    gather_wide = Gather(place, wide_all, wide_send, wide_recv)
    wide_events = gather_wide.events()
    wide_events[0]()

    gather_grads.rest()
    loads[8].wait()
    toward = 1 - 2 * core
    ahead = mod(z + toward, PLANES)
    behind = mod(z - toward, PLANES)

    def partial(offset):
        source = mod(z + toward * offset, PLANES)
        total = None
        for j in range(4):
            slot = device_of(z, j // 2, j % 2, source)
            term = jnp.dot(
                grads_all[slot], bout_v[pl.ds(j * HID, HID), :], preferred_element_type=F32
            )
            total = term if total is None else total + term
        return total

    z_sent = []

    def hop(kept, landing, sends, recvs, step, target):
        copy = pltpu.make_async_remote_copy(
            src_ref=kept.at[step],
            dst_ref=landing.at[step],
            send_sem=sends.at[step],
            recv_sem=recvs.at[step],
            device_id=(target, m),
            device_id_type=MESH,
        )
        copy.start()
        z_sent.append(copy)
        return copy

    hop_a = functools.partial(hop, send_a, got_a, a_send, a_recv)
    hop_b = functools.partial(hop, send_b, got_b, b_send, b_recv)
    send_a[0] = partial(4).astype(BF16)
    last_a = hop_a(0, ahead)
    send_b[0] = partial(-3).astype(BF16)
    last_b = hop_b(0, behind)
    wide_queue = wide_events[1:]

    def serve(n):
        for _ in range(n):
            if wide_queue:
                wide_queue.pop(0)()

    for step in (1, 2, 3):
        mine = partial(4 - step)
        serve(2)
        last_a.wait_recv()
        send_a[step] = (mine + got_a[step - 1].astype(F32)).astype(BF16)
        last_a = hop_a(step, ahead)
        if step < 3:
            mine = partial(step - 3)
            serve(2)
            last_b.wait_recv()
            send_b[step] = (mine + got_b[step - 1].astype(F32)).astype(BF16)
            last_b = hop_b(step, behind)
    mine = partial(0)
    serve(len(wide_queue))
    last_b.wait_recv()
    last_a.wait_recv()
    mine = mine + got_b[2].astype(F32) + got_a[3].astype(F32)
    qout_all[pl.ds(pl.multiple_of(z * RANK, RANK), RANK), :] = mine[TOKENS:].astype(BF16)
    qout_sent = []
    for o in range(1, PLANES):
        rows = pl.ds(pl.multiple_of(z * RANK, RANK), RANK)
        copy = pltpu.make_async_remote_copy(
            src_ref=qout_all.at[rows],
            dst_ref=qout_all.at[rows],
            send_sem=qout_send.at[o],
            recv_sem=qout_recv.at[o],
            device_id=(mod(z + o, PLANES), m),
            device_id_type=MESH,
        )
        copy.start()
        qout_sent.append(copy)
    pad[...] = jnp.zeros_like(pad)
    for s in range(2):
        pad[pl.ds(0, LEN), pl.ds(0, HID)] = mine[s * LEN : (s + 1) * LEN]
        left[s] = pad[...].T.astype(BF16)

    gather_wide.rest()
    mixed[...] = jnp.zeros_like(mixed)

    def score(slot, carry):
        columns = pl.ds(pl.multiple_of(slot * FEAT, FEAT), FEAT)
        inverse = 1.0 / (eig_v[:, columns].astype(F32) + damping)
        queries = wide_all[slot, pl.ds(TOKENS, QROWS), :]
        for s in range(2):
            outer = jnp.dot(
                left[s, pl.ds(0, HID), :],
                wide_all[slot, pl.ds(s * LEN, 128), :],
                preferred_element_type=F32,
            )
            weighted = (outer * inverse).astype(BF16)
            mixed[s] += lax.dot_general(
                weighted, queries, (((1,), (1,)), ((), ())), preferred_element_type=F32
            )
        return carry

    lax.fori_loop(0, DEVICES, score, 0)
    for copy in qout_sent:
        copy.wait_recv()
    pad[:, pl.ds(0, HID)] = qout_all[...].astype(F32)
    qout_t[...] = pad[...].T
    tiles2[0] = jnp.zeros((8, 128), F32)
    for s in range(2):
        tiles2[0, pl.ds(s, 1), :] = jnp.sum(
            mixed[s] * qout_t[pl.ds(0, HID), :], axis=0, keepdims=True
        )
    total, sum2_sent = plane_sum(place, tiles2, landed2, sum2_send, sum2_recv)
    out[...] = total

    for gather in (gather_acts, gather_grads, gather_wide):
        gather.finish()
    for copy in qin_sent + qout_sent + z_sent + sum1_sent + sum2_sent:
        copy.wait_send()


def per_device(
    activations, out_grads, valid_counts, basis_in, basis_out, eigvals, query_out, query_in
):
    anywhere = pl.BlockSpec(memory_space=pl.ANY)
    dma = pltpu.SemaphoreType.DMA
    summed = pl.pallas_call(
        kernel,
        out_shape=jax.ShapeDtypeStruct((8, 128), F32),
        in_specs=[anywhere, anywhere, pl.BlockSpec(memory_space=pltpu.SMEM)] + [anywhere] * 5,
        out_specs=pl.BlockSpec(memory_space=pltpu.VMEM),
        scratch_shapes=[
            pltpu.VMEM((D, FEAT), BF16),
            pltpu.VMEM((4 * HID, HID), BF16),
            pltpu.VMEM((HID, D), BF16),
            pltpu.VMEM((DEVICES, ROWS, FEAT), BF16),
            pltpu.VMEM((ROWS, HID), BF16),
            pltpu.VMEM((DEVICES, ROWS, HID), BF16),
            pltpu.VMEM((DEVICES, WIDE, FEAT), BF16),
            pltpu.VMEM((ROWS, FEAT), F32),
            pltpu.VMEM((4, ROWS, HID), BF16),
            pltpu.VMEM((3, ROWS, HID), BF16),
            pltpu.VMEM((4, ROWS, HID), BF16),
            pltpu.VMEM((3, ROWS, HID), BF16),
            pltpu.VMEM((QROWS, HID), BF16),
            pltpu.VMEM((128, 512), F32),
            pltpu.VMEM((2, 512, 128), BF16),
            pltpu.VMEM((512, 128), F32),
            pltpu.VMEM((2, HID, QROWS), F32),
            pltpu.VMEM((3, 8, 128), F32),
            pltpu.VMEM((7, 8, 128), F32),
            pltpu.VMEM((3, 8, 128), F32),
            pltpu.VMEM((7, 8, 128), F32),
            dma((9,)),
            dma((31,)),
            dma((32,)),
            dma((31,)),
            dma((32,)),
            dma((31,)),
            dma((32,)),
            dma((3,)),
            dma((8,)),
            dma((8,)),
            dma((8,)),
            dma((8,)),
            dma((4,)),
            dma((4,)),
            dma((3,)),
            dma((3,)),
            dma((7,)),
            dma((7,)),
            dma((7,)),
            dma((7,)),
        ],
        compiler_params=pltpu.CompilerParams(
            collective_id=0, has_side_effects=True, vmem_limit_bytes=56 * 1024 * 1024
        ),
    )(activations, out_grads, valid_counts, basis_in, basis_out, eigvals, query_out, query_in)
    return jnp.sum(summed[:2].reshape(2, PLANES, RANK), axis=2)


def solution(mesh):
    in_specs = (
        P("grp", None, "mp"),
        P("grp", None, "mp"),
        P("grp"),
        P(None, "mp"),
        P("grp", "mp"),
        P("mp", None),
        P("grp", None, "mp"),
        P("grp", None, "mp"),
    )
    return jax.shard_map(
        per_device, mesh=mesh, in_specs=in_specs, out_specs=P("grp", None), check_vma=False
    )
```

time: 447 us -> 136 us (0.30)
  blocking collectives: 211 us -> 0 us
  waiting for transfers between devices: 149 us -> 0 us
  Pallas kernels: 0 us -> 130 us
  matrix products: 30.8 us -> 0 us
  local copies, waits for them, and re-layouts: 32.5 us -> 4.52 us
  between operations: 13.9 us -> 0.01 us
  other arithmetic: 9.19 us -> 0.66 us
    all_gather x5 -> x0, waiting for transfers between devices: 147 us -> none  [the longest x1 56.5 us: per_device(): lax.all_gather(basis_out, 'grp', axis=0, tiled=True)]
    pallas_call x0 -> x1, Pallas kernels: none -> 130 us  [per_device(): pl.pallas_call(kernel, out_shape=jax.ShapeDtypeStruct((8, 128), F32), in_...]
    psum x2 -> x0, blocking collectives: 130 us -> none  [the longest x1 66.4 us: per_device(): return lax.psum(partial_scores, 'mp')]
    all_gather x3 -> x0, blocking collectives: 81.3 us -> none  [the longest x1 35.3 us: per_device(): lax.all_gather(query_out, 'mp', axis=2, tiled=True)]
    dot_general x4 -> x0, matrix products: 30.8 us -> none  [the longest x2 16.6 us: per_device(): lax.dot_general(weighted, qin_flat, (((1,), (1,)), ((), ())), preferred_e...]
    all_gather x2 -> x0, local copies, waits for them, and re-layouts: 29.5 us -> none  [the longest x1 16 us: per_device(): lax.all_gather(out_grads, 'mp', axis=2, tiled=True)]
    reduce_sum x3 -> x1, other arithmetic: 7.7 us -> 0.66 us  [per_device(): return jnp.sum(summed[:2].reshape(2, PLANES, RANK), axis=2)]
  transfers between devices with their start and end apart: 5 -> 0, of which waited for: 4 -> 0; matrix products, arithmetic and copies ran while one was open for 11% -> 0% of each run, Pallas kernels for 0% -> 0%
where the time goes in v1:
time: 136 us
  Pallas kernels  130 us (96%)
  local copies, waits for them, and re-layouts  4.52 us (3%)
    pallas_call x1, Pallas kernels, per_device(): pl.pallas_call(kernel, out_shape=jax.ShapeDtypeStruct((8, 128), F32), in_...  130 us
    unnamed x1, local copies, waits for them, and re-layouts  3.76 us

profile of v1, /device:TPU:1, one launch (start us, length us, event | category | flops | bytes accessed | tf_op | source)
XLA Modules:
  0.0 135.5 jit_solution(14686522948722476369)
XLA Ops:
  0.0 3.8 %copy.9.basis_out = bf16[1792,448]{1,0:T(8,128)(2,1)} copy(bf16[1792,448]{0,1:T(8,128)(2,1)} %param.12) | data formatting | bytes 3211264 | tf_op args[4]
  3.8 130.3 %shard_map.82 = f32[8,128]{1,0:T(8,128)} custom-call(bf16[2,96,256]{2,1,0:T(8,128)(2,1)} %acts.1, bf16[2,96,448]{2,1,0:T(8,128)(2,1)} %grads.1, s32[2]{0:T(128)} %counts.1, bf16[8192,256]{1,0:T(8,128)(2,1)} %basis_in.1, bf16[1792,448]{1,0:T(8,128)(2,1)} %copy.9.basis_out, bf16[448,8192]{1,0:T(8,128)(2,1)} %eigvals.1, bf16[1,16,448]{2,1,0:T(8,128)(2,1)} %query_out.1, ...), custom_call_target="tpu_custom_call" | custom-call | tf_op jit(solution)/shard_map/pallas_call | solution.py:471
  134.1 0.7 slice.3
  134.8 0.1 reshape.3
  134.9 0.7 reduce_sum.9

commit v2 on v1

v2 whole, which is shorter than its diff:
```python
import functools

import jax
import jax.numpy as jnp
from jax import lax
from jax.experimental import pallas as pl
from jax.experimental.pallas import tpu as pltpu
from jax.sharding import PartitionSpec as P

MESH = pl.DeviceIdType.MESH
F32 = jnp.float32
BF16 = jnp.bfloat16

SIDE = 4
PLANES = 8
DEVICES = 32
TOKENS = 192
RANK = 16
ROWS = TOKENS + RANK
LEN = 96
HID = 448
FEAT = 256
QROWS = PLANES * RANK
WIDE = TOKENS + QROWS
FF = HID * DEVICES
D = FEAT * DEVICES


def mod(value, n):
    return lax.rem(value + 2 * n, n)


class Gather:
    def __init__(self, place, buf, send_sems, recv_sems):
        self.z, self.m, self.x, self.y, self.core = place
        self.buf, self.send_sems, self.recv_sems = buf, send_sems, recv_sems
        self.p1 = self.x * (1 - self.core) + self.y * self.core
        self.p2 = self.y * (1 - self.core) + self.x * self.core
        self.sibling = self.m + 1 - 2 * self.core
        self.sent = []

    def slot(self, d1, d2):
        a, b = mod(self.p1 + d1, SIDE), mod(self.p2 + d2, SIDE)
        x = a * (1 - self.core) + b * self.core
        y = b * (1 - self.core) + a * self.core
        return (x * SIDE + y) * 2 + self.core

    def copy(self, slot, to, index):
        return pltpu.make_async_remote_copy(
            src_ref=self.buf.at[slot],
            dst_ref=self.buf.at[slot],
            send_sem=self.send_sems.at[index],
            recv_sem=self.recv_sems.at[slot],
            device_id=(self.z, to),
            device_id_type=MESH,
        )

    def send(self, slot, to):
        copy = self.copy(slot, to, len(self.sent))
        copy.start()
        self.sent.append(copy)

    def arrive(self, slot):
        self.copy(slot, self.sibling, 0).wait_recv()

    def event(self, offset, first=(), second=()):
        slot = self.slot(*offset)
        if offset != (0, 0):
            self.arrive(slot)
        for step in first:
            self.send(slot, self.slot(step, 0))
        for step in second:
            self.send(slot, self.slot(0, step))
        self.send(slot, self.sibling)

    def events(self):
        both = (1, -1)
        plan = [
            ((0, 0), both, both),
            ((-1, 0), (1,), both),
            ((1, 0), (), both),
            ((0, -1), (), (1,)),
            ((0, 1), (), ()),
            ((2, 0), (), both),
            ((-1, -1), (), ()),
            ((-1, 1), (), (-1,)),
            ((1, -1), (), ()),
            ((1, 1), (), (-1,)),
            ((2, -1), (), (1,)),
            ((2, 1), (), ()),
            ((0, 2), (), ()),
            ((-1, 2), (), ()),
            ((1, 2), (), ()),
            ((2, 2), (), ()),
        ]
        return [functools.partial(self.event, *entry) for entry in plan]

    def rest(self):
        def body(chip, carry):
            self.arrive(chip * 2 + 1 - self.core)
            return carry

        lax.fori_loop(0, SIDE * SIDE, body, 0)

    def finish(self):
        for copy in self.sent:
            copy.wait_send()


def plane_sum(place, tiles, landed, send_sems, recv_sems):
    z = place[0]
    row, column = sum_peers(place)
    sent = []

    def exchange(stage, base, peers):
        for index, peer in enumerate(peers):
            copy = pltpu.make_async_remote_copy(
                src_ref=tiles.at[stage],
                dst_ref=landed.at[base + index],
                send_sem=send_sems.at[base + index],
                recv_sem=recv_sems.at[base + index],
                device_id=(z, peer),
                device_id_type=MESH,
            )
            copy.start()
            sent.append(copy)

    def collect(stage, base, peers):
        total = tiles[stage]
        for index in range(len(peers)):
            sent[base + index].wait_recv()
            total = total + landed[base + index]
        return total

    def first():
        exchange(0, 0, row)

    def second():
        tiles[1] = collect(0, 0, row)
        exchange(1, len(row), column)

    def last():
        return collect(1, len(row), column)

    return first, second, last, sent


def sum_peers(place):
    z, m, x, y, core = place
    row = []
    for ox in range(SIDE):
        for oc in range(2):
            if ox or oc:
                row.append((mod(x + ox, SIDE) * SIDE + y) * 2 + lax.rem(core + oc, 2))
    column = [(x * SIDE + mod(y + o, SIDE)) * 2 + core for o in (1, 2, 3)]
    return row, column


HALF = (LEN, LEN + RANK)


def kernel(
    acts,
    grads,
    counts,
    basis_in,
    basis_out,
    eigvals,
    query_out,
    query_in,
    out,
    bin_v,
    bout_t,
    bout_v,
    eig_v,
    inverse,
    acts_all,
    stage0,
    stage1,
    relay0,
    relay1,
    grads0,
    grads1,
    wide_all,
    acc_in,
    send_a0,
    send_b0,
    got_a0,
    got_b0,
    send_a1,
    send_b1,
    got_a1,
    got_b1,
    mine0,
    mine1,
    qout_all,
    pad,
    left,
    qout_t,
    mixed,
    tiles1,
    landed1,
    tiles2,
    landed2,
    local_sems,
    acts_send,
    acts_recv,
    grads_send0,
    grads_recv0,
    grads_send1,
    grads_recv1,
    wide_send,
    wide_recv,
    perm_sems,
    qin_send,
    qin_recv,
    qout_send,
    qout_recv,
    z_send,
    z_recv,
    sum1_send,
    sum1_recv,
    sum2_send,
    sum2_recv,
):
    z = lax.axis_index("grp")
    m = lax.axis_index("mp")
    core = lax.rem(m, 2)
    chip = lax.div(m, 2)
    x, y = lax.div(chip, SIDE), lax.rem(chip, SIDE)
    place = (z, m, x, y, core)
    stage, relay, grads_all = (stage0, stage1), (relay0, relay1), (grads0, grads1)

    loads = []

    def load(src, dst):
        copy = pltpu.make_async_copy(src, dst, local_sems.at[len(loads)])
        copy.start()
        loads.append(copy)

    load(grads.at[0], stage0)
    load(grads.at[1], stage1.at[pl.ds(0, LEN)])
    load(query_out.at[0], stage1.at[pl.ds(LEN, RANK)])
    load(acts.at[0], acts_all.at[m, pl.ds(0, LEN)])
    load(acts.at[1], acts_all.at[m, pl.ds(LEN, LEN)])
    load(query_in.at[0], acts_all.at[m, pl.ds(TOKENS, RANK)])
    load(eigvals, eig_v)
    load(basis_out, bout_t.at[pl.ds(0, HID)])
    load(basis_in, bin_v)

    y_low, y_high = lax.rem(y, 2), lax.div(y, 2)

    def place_of(target, j_high, j_low, source):
        ring = mod(target - source - 4 * j_low, PLANES)
        high = lax.rem(ring, 2)
        low = lax.rem(j_high + lax.rem(target, 2) + high, 2)
        return (lax.div(ring, 2) * SIDE + 2 * high + low) * 2 + j_low

    x_relay = lax.div(mod(2 * x + y_high - z - 4 * core, PLANES), 2)
    relay_to = (x_relay * SIDE + y) * 2 + core
    ring = 2 * x + lax.rem(y_high + z, 2)
    plane = lax.rem(ring + z + 4 * core, PLANES)
    to = place_of(plane, y_low, core, z)
    from_plane = mod(z - (2 * x + y_high) - 4 * core, PLANES)
    from_y = 2 * lax.rem(z, 2) + lax.rem(y_low + y_high + lax.rem(z, 2), 2)
    from_device = (x * SIDE + from_y) * 2 + core
    shifts = x_relay != x
    stays = jnp.logical_and(plane == z, to == m)
    moves = jnp.logical_not(stays)

    barrier = pltpu.get_barrier_semaphore()
    row, column = sum_peers(place)
    for peer in row + column:
        pl.semaphore_signal(barrier, inc=1, device_id=(z, peer), device_id_type=MESH)
    for o in range(1, PLANES):
        pl.semaphore_signal(
            barrier, inc=1, device_id=(mod(z + o, PLANES), m), device_id_type=MESH
        )

    @pl.when(moves)
    def _():
        pl.semaphore_signal(
            barrier, inc=1, device_id=(from_plane, from_device), device_id_type=MESH
        )

    pl.semaphore_wait(
        barrier, len(row) + len(column) + PLANES - 1 + jnp.where(stays, 0, 1)
    )

    shift, shift_here, permute, permute_here = [], [], [], []
    for h in range(2):
        shift.append(
            pltpu.make_async_remote_copy(
                src_ref=stage[h],
                dst_ref=relay[h],
                send_sem=perm_sems.at[h],
                recv_sem=perm_sems.at[2 + h],
                device_id=(z, relay_to),
                device_id_type=MESH,
            )
        )
        shift_here.append(pltpu.make_async_copy(stage[h], relay[h], perm_sems.at[4 + h]))
        permute.append(
            pltpu.make_async_remote_copy(
                src_ref=relay[h],
                dst_ref=grads_all[h].at[to],
                send_sem=perm_sems.at[6 + h],
                recv_sem=perm_sems.at[8 + h],
                device_id=(plane, to),
                device_id_type=MESH,
            )
        )
        permute_here.append(
            pltpu.make_async_copy(relay[h], grads_all[h].at[m], perm_sems.at[10 + h])
        )

    def one_of(predicate, yes, no):
        @pl.when(predicate)
        def _():
            yes()

        @pl.when(jnp.logical_not(predicate))
        def _():
            no()

    for copy in loads[:3]:
        copy.wait()
    for h in range(2):
        one_of(shifts, shift[h].start, shift_here[h].start)
    for copy in loads[3:6]:
        copy.wait()
    gather_acts = Gather(place, acts_all, acts_send, acts_recv)
    gather_grads = [
        Gather(place, grads0, grads_send0, grads_recv0),
        Gather(place, grads1, grads_send1, grads_recv1),
    ]
    gather_wide = Gather(place, wide_all, wide_send, wide_recv)
    acts_queue = gather_acts.events()
    grads_queue = [gather.events() for gather in gather_grads]
    wide_queue = gather_wide.events()

    def serve(queue, n):
        for _ in range(n):
            if queue:
                queue.pop(0)()

    serve(acts_queue, 1)
    for h in range(2):
        one_of(shifts, shift[h].wait, shift_here[h].wait)
        one_of(moves, permute[h].start, permute_here[h].start)

    sum_first, sum_second, sum_last, sum1_sent = plane_sum(
        place, tiles1, landed1, sum1_send, sum1_recv
    )

    def sum_eig():
        loads[6].wait()

        def add_eig(slot, total):
            columns = pl.ds(pl.multiple_of(slot * FEAT, FEAT), FEAT)
            block = eig_v[:, columns].astype(F32).reshape(HID // 8, 8, FEAT)
            return total + jnp.sum(block, axis=0)

        eig_sum = lax.fori_loop(0, DEVICES, add_eig, jnp.zeros((8, FEAT), F32))
        tiles1[0] = eig_sum[:, :128] + eig_sum[:, 128:]
        sum_first()

    def turn_basis():
        loads[7].wait()

        def turn(i, carry):
            rows = pl.ds(pl.multiple_of(i * 128, 128), 128)
            turned = bout_t[:, rows].astype(F32).T
            bout_v[rows, :] = turned[:, :HID].astype(BF16)
            return carry

        lax.fori_loop(0, 4 * HID // 128, turn, 0)

    def invert(start, stop):
        def body(slot, carry):
            columns = pl.ds(pl.multiple_of(slot * FEAT, FEAT), FEAT)
            inverse[slot] = 1.0 / (eig_v[:, columns].astype(F32) + damping)
            return carry

        lax.fori_loop(start, stop, body, 0)

    qin_sent = []
    my_query = pl.ds(pl.multiple_of(TOKENS + z * RANK, RANK), RANK)

    def rotate_in():
        gather_acts.rest()
        loads[8].wait()
        acc_in[...] = jnp.zeros_like(acc_in)

        def body(slot, carry):
            rows = pl.ds(pl.multiple_of(slot * FEAT, FEAT), FEAT)
            acc_in[...] += jnp.dot(acts_all[slot], bin_v[rows, :], preferred_element_type=F32)
            return carry

        lax.fori_loop(0, DEVICES, body, 0)
        position = lax.broadcasted_iota(jnp.int32, (LEN, FEAT), 0)
        for s in range(2):
            rows = pl.ds(s * LEN, LEN)
            kept = jnp.where(position < counts[s], acc_in[rows, :], 0.0)
            wide_all[m, rows, :] = kept.astype(BF16)
        wide_all[m, my_query, :] = acc_in[pl.ds(TOKENS, RANK), :].astype(BF16)
        for o in range(1, PLANES):
            copy = pltpu.make_async_remote_copy(
                src_ref=wide_all.at[m, my_query],
                dst_ref=wide_all.at[m, my_query],
                send_sem=qin_send.at[o],
                recv_sem=qin_recv.at[o],
                device_id=(mod(z + o, PLANES), m),
                device_id_type=MESH,
            )
            copy.start()
            qin_sent.append(copy)

    toward = 1 - 2 * core
    ahead = mod(z + toward, PLANES)
    behind = mod(z - toward, PLANES)
    kept_a, kept_b = (send_a0, send_a1), (send_b0, send_b1)
    landed_a, landed_b = (got_a0, got_a1), (got_b0, got_b1)
    mine = (mine0, mine1)
    z_sent = []
    last = {}

    def pair(h, offsets):
        total = None
        slots = [mod(z + toward * offset, PLANES) for offset in offsets]
        for j in range(4):
            lhs = [grads_all[h][place_of(z, j // 2, j % 2, source)] for source in slots]
            term = jnp.dot(
                jnp.concatenate(lhs, axis=0),
                bout_v[pl.ds(j * HID, HID), :],
                preferred_element_type=F32,
            )
            total = term if total is None else total + term
        return total[: HALF[h]], total[HALF[h] :]

    def hop(h, way, step):
        index = h * 7 + way * 4 + step
        copy = pltpu.make_async_remote_copy(
            src_ref=(kept_a, kept_b)[way][h].at[step],
            dst_ref=(landed_a, landed_b)[way][h].at[step],
            send_sem=z_send.at[index],
            recv_sem=z_recv.at[index],
            device_id=((ahead, behind)[way], m),
            device_id_type=MESH,
        )
        copy.start()
        z_sent.append(copy)
        last[h, way] = copy

    def reduce_step(h, step):
        if step == 0:
            a, b = pair(h, (4, -3))
            kept_a[h][0] = a.astype(BF16)
            hop(h, 0, 0)
            kept_b[h][0] = b.astype(BF16)
            hop(h, 1, 0)
        elif step < 3:
            a, b = pair(h, (4 - step, step - 3))
            last[h, 0].wait_recv()
            kept_a[h][step] = (a + landed_a[h][step - 1].astype(F32)).astype(BF16)
            hop(h, 0, step)
            last[h, 1].wait_recv()
            kept_b[h][step] = (b + landed_b[h][step - 1].astype(F32)).astype(BF16)
            hop(h, 1, step)
        elif step == 3:
            a, b = pair(h, (1, 0))
            last[h, 0].wait_recv()
            kept_a[h][3] = (a + landed_a[h][2].astype(F32)).astype(BF16)
            hop(h, 0, 3)
            last[h, 1].wait_recv()
            mine[h][...] = b + landed_b[h][2].astype(F32)
        else:
            last[h, 0].wait_recv()
            mine[h][...] += landed_a[h][3].astype(F32)
            pad[pl.ds(0, LEN), pl.ds(0, HID)] = mine[h][pl.ds(0, LEN), :]
            left[h] = pad[...].T.astype(BF16)

    pad[...] = jnp.zeros_like(pad)
    serve(acts_queue, 5)
    sum_eig()
    serve(acts_queue, 4)
    for h in range(2):
        one_of(moves, permute[h].wait, permute_here[h].wait)
        serve(grads_queue[h], 1)
    serve(acts_queue, 6)
    serve(grads_queue[0], 5)
    sum_second()
    turn_basis()
    serve(grads_queue[0], 4)
    rotate_in()
    serve(grads_queue[0], 6)
    serve(grads_queue[1], 5)
    damping = 0.1 * jnp.sum(sum_last()) / (FF * D)
    gather_grads[0].rest()
    reduce_step(0, 0)
    serve(grads_queue[1], 4)
    invert(0, 8)
    reduce_step(0, 1)
    serve(grads_queue[1], 3)
    for copy in qin_sent:
        copy.wait_recv()
    serve(wide_queue, 1)
    serve(grads_queue[1], 3)
    reduce_step(0, 2)
    serve(wide_queue, 2)
    gather_grads[1].rest()
    reduce_step(1, 0)
    serve(wide_queue, 3)
    reduce_step(0, 3)
    invert(8, 16)
    reduce_step(1, 1)
    serve(wide_queue, 3)
    reduce_step(0, 4)
    invert(16, 24)
    reduce_step(1, 2)
    serve(wide_queue, 4)
    invert(24, 32)
    reduce_step(1, 3)
    serve(wide_queue, 3)
    reduce_step(1, 4)

    my_rows = pl.ds(pl.multiple_of(z * RANK, RANK), RANK)
    qout_all[my_rows, :] = mine1[pl.ds(LEN, RANK), :].astype(BF16)
    qout_sent = []
    for o in range(1, PLANES):
        copy = pltpu.make_async_remote_copy(
            src_ref=qout_all.at[my_rows],
            dst_ref=qout_all.at[my_rows],
            send_sem=qout_send.at[o],
            recv_sem=qout_recv.at[o],
            device_id=(mod(z + o, PLANES), m),
            device_id_type=MESH,
        )
        copy.start()
        qout_sent.append(copy)

    gather_wide.rest()
    mixed[...] = jnp.zeros_like(mixed)

    def score(slot, carry):
        queries = wide_all[slot, pl.ds(TOKENS, QROWS), :]
        for s in range(2):
            outer = jnp.dot(
                left[s, pl.ds(0, HID), :],
                wide_all[slot, pl.ds(s * LEN, 128), :],
                preferred_element_type=F32,
            )
            weighted = (outer * inverse[slot]).astype(BF16)
            mixed[s] += lax.dot_general(
                weighted, queries, (((1,), (1,)), ((), ())), preferred_element_type=F32
            )
        return carry

    lax.fori_loop(0, DEVICES, score, 0)
    for copy in qout_sent:
        copy.wait_recv()
    pad[:, pl.ds(0, HID)] = qout_all[...].astype(F32)
    qout_t[...] = pad[...].T
    tiles2[0] = jnp.zeros((8, 128), F32)
    for s in range(2):
        tiles2[0, pl.ds(s, 1), :] = jnp.sum(
            mixed[s] * qout_t[pl.ds(0, HID), :], axis=0, keepdims=True
        )
    end_first, end_second, end_last, sum2_sent = plane_sum(
        place, tiles2, landed2, sum2_send, sum2_recv
    )
    end_first()
    end_second()
    out[...] = end_last()[:2]

    for gather in (gather_acts, *gather_grads, gather_wide):
        gather.finish()
    for copy in qin_sent + qout_sent + z_sent + sum1_sent + sum2_sent:
        copy.wait_send()


def per_device(
    activations, out_grads, valid_counts, basis_in, basis_out, eigvals, query_out, query_in
):
    anywhere = pl.BlockSpec(memory_space=pl.ANY)
    dma = pltpu.SemaphoreType.DMA
    halves = [
        pltpu.VMEM((count, rows, HID), BF16)
        for rows in HALF
        for count in (4, 3, 4, 3)
    ]
    gather_sems = [dma((31,)), dma((32,))]
    summed = pl.pallas_call(
        kernel,
        out_shape=jax.ShapeDtypeStruct((2, 128), F32),
        in_specs=[anywhere, anywhere, pl.BlockSpec(memory_space=pltpu.SMEM)] + [anywhere] * 5,
        out_specs=pl.BlockSpec(memory_space=pltpu.VMEM),
        scratch_shapes=[
            pltpu.VMEM((D, FEAT), BF16),
            pltpu.VMEM((512, 4 * HID), BF16),
            pltpu.VMEM((4 * HID, HID), BF16),
            pltpu.VMEM((HID, D), BF16),
            pltpu.VMEM((DEVICES, HID, FEAT), F32),
            pltpu.VMEM((DEVICES, ROWS, FEAT), BF16),
            pltpu.VMEM((HALF[0], HID), BF16),
            pltpu.VMEM((HALF[1], HID), BF16),
            pltpu.VMEM((HALF[0], HID), BF16),
            pltpu.VMEM((HALF[1], HID), BF16),
            pltpu.VMEM((DEVICES, HALF[0], HID), BF16),
            pltpu.VMEM((DEVICES, HALF[1], HID), BF16),
            pltpu.VMEM((DEVICES, WIDE, FEAT), BF16),
            pltpu.VMEM((ROWS, FEAT), F32),
            *halves,
            pltpu.VMEM((HALF[0], HID), F32),
            pltpu.VMEM((HALF[1], HID), F32),
            pltpu.VMEM((QROWS, HID), BF16),
            pltpu.VMEM((128, 512), F32),
            pltpu.VMEM((2, 512, 128), BF16),
            pltpu.VMEM((512, 128), F32),
            pltpu.VMEM((2, HID, QROWS), F32),
            pltpu.VMEM((2, 8, 128), F32),
            pltpu.VMEM((10, 8, 128), F32),
            pltpu.VMEM((2, 8, 128), F32),
            pltpu.VMEM((10, 8, 128), F32),
            dma((9,)),
            *gather_sems * 4,
            dma((12,)),
            dma((8,)),
            dma((8,)),
            dma((8,)),
            dma((8,)),
            dma((14,)),
            dma((14,)),
            dma((10,)),
            dma((10,)),
            dma((10,)),
            dma((10,)),
        ],
        compiler_params=pltpu.CompilerParams(
            collective_id=0, has_side_effects=True, vmem_limit_bytes=60 * 1024 * 1024
        ),
    )(activations, out_grads, valid_counts, basis_in, basis_out.T, eigvals, query_out, query_in)
    return jnp.sum(summed.reshape(2, PLANES, RANK), axis=2)


def solution(mesh):
    in_specs = (
        P("grp", None, "mp"),
        P("grp", None, "mp"),
        P("grp"),
        P(None, "mp"),
        P("grp", "mp"),
        P("mp", None),
        P("grp", None, "mp"),
        P("grp", None, "mp"),
    )
    return jax.shard_map(
        per_device, mesh=mesh, in_specs=in_specs, out_specs=P("grp", None), check_vma=False
    )
```

time: 136 us -> 116 us (0.85)
  Pallas kernels: 130 us -> 115 us
  local copies, waits for them, and re-layouts: 4.52 us -> 0.76 us
    pallas_call x1, Pallas kernels: 130 us -> 115 us  [per_device(): pl.pallas_call(kernel, out_shape=jax.ShapeDtypeStruct((2, 128), F32), in_...]
    unnamed x1 -> x0, local copies, waits for them, and re-layouts: 3.76 us -> none
where the time goes in v2:
time: 116 us
  Pallas kernels  115 us (99%)
    pallas_call x1, Pallas kernels, per_device(): pl.pallas_call(kernel, out_shape=jax.ShapeDtypeStruct((2, 128), F32), in_...  115 us

profile of v2, /device:TPU:1, one launch (start us, length us, event | category | flops | bytes accessed | tf_op | source)
XLA Modules:
  0.0 116.1 jit_solution(18300239090043505818)
XLA Ops:
  0.0 114.7 %shard_map.82 = f32[2,128]{1,0:T(2,128)} custom-call(bf16[2,96,256]{2,1,0:T(8,128)(2,1)} %acts.1, bf16[2,96,448]{2,1,0:T(8,128)(2,1)} %grads.1, s32[2]{0:T(128)} %counts.1, bf16[8192,256]{1,0:T(8,128)(2,1)} %basis_in.1, bf16[448,1792]{1,0:T(8,128)(2,1)} %bitcast.1, bf16[448,8192]{1,0:T(8,128)(2,1)} %eigvals.1, bf16[1,16,448]{2,1,0:T(8,128)(2,1)} %query_out.1, ...), custom_call_target="tpu_custom_call" | custom-call | tf_op jit(solution)/shard_map/pallas_call | solution.py:593
  114.7 0.8 reshape.3
  115.4 0.7 reduce_sum.9

commit v3 on v2

--- a/solution.py
+++ b/solution.py
@@ -30,20 +30,44 @@
     return lax.rem(value + 2 * n, n)
 
 
+BOTH = (1, -1)
+RING = (
+    ((0, 0), BOTH, BOTH),
+    ((-1, 0), (1,), BOTH),
+    ((1, 0), (), BOTH),
+    ((0, -1), (), (1,)),
+    ((0, 1), (), ()),
+    ((2, 0), (), BOTH),
+    ((-1, -1), (), ()),
+    ((-1, 1), (), (-1,)),
+    ((1, -1), (), ()),
+    ((1, 1), (), (-1,)),
+    ((2, -1), (), (1,)),
+    ((2, 1), (), ()),
+    ((0, 2), (), ()),
+    ((-1, 2), (), ()),
+    ((1, 2), (), ()),
+    ((2, 2), (), ()),
+)
+EARLY = (((0, 0), (1, -1, 2), BOTH), ((-1, 0), (), BOTH)) + RING[2:]
+GROUPS = (0, -1, 1, 2)
+
+
+def slot_of(x, y, core, d1, d2):
+    a = mod(x * (1 - core) + y * core + d1, SIDE)
+    b = mod(y * (1 - core) + x * core + d2, SIDE)
+    return ((a * (1 - core) + b * core) * SIDE + b * (1 - core) + a * core) * 2 + core
+
+
 class Gather:
     def __init__(self, place, buf, send_sems, recv_sems):
         self.z, self.m, self.x, self.y, self.core = place
         self.buf, self.send_sems, self.recv_sems = buf, send_sems, recv_sems
-        self.p1 = self.x * (1 - self.core) + self.y * self.core
-        self.p2 = self.y * (1 - self.core) + self.x * self.core
         self.sibling = self.m + 1 - 2 * self.core
         self.sent = []
 
     def slot(self, d1, d2):
-        a, b = mod(self.p1 + d1, SIDE), mod(self.p2 + d2, SIDE)
-        x = a * (1 - self.core) + b * self.core
-        y = b * (1 - self.core) + a * self.core
-        return (x * SIDE + y) * 2 + self.core
+        return slot_of(self.x, self.y, self.core, d1, d2)
 
     def copy(self, slot, to, index):
         return pltpu.make_async_remote_copy(
@@ -73,27 +97,15 @@
             self.send(slot, self.slot(0, step))
         self.send(slot, self.sibling)
 
-    def events(self):
-        both = (1, -1)
-        plan = [
-            ((0, 0), both, both),
-            ((-1, 0), (1,), both),
-            ((1, 0), (), both),
-            ((0, -1), (), (1,)),
-            ((0, 1), (), ()),
-            ((2, 0), (), both),
-            ((-1, -1), (), ()),
-            ((-1, 1), (), (-1,)),
-            ((1, -1), (), ()),
-            ((1, 1), (), (-1,)),
-            ((2, -1), (), (1,)),
-            ((2, 1), (), ()),
-            ((0, 2), (), ()),
-            ((-1, 2), (), ()),
-            ((1, 2), (), ()),
-            ((2, 2), (), ()),
-        ]
+    def events(self, plan):
         return [functools.partial(self.event, *entry) for entry in plan]
+
+    def group(self, d1):
+        def body(d2, carry):
+            self.arrive(slot_of(self.x, self.y, 1 - self.core, d1, d2))
+            return carry
+
+        lax.fori_loop(0, SIDE, body, 0)
 
     def rest(self):
         def body(chip, carry):
@@ -156,6 +168,18 @@
     return row, column
 
 
+PLAN_A, PLAN_G, PLAN_W = RING, EARLY, RING
+SCHEDULE = (
+    "sG", "sH", "A0", "turn", "eig", "rG", "rH", "A1", "A2", "A3", "A4", "eig2", "A5", "A7",
+    "tG", "G0", "A6", "A9", "A8", "A12", "damp", "tH", "H0", "A11", "A10", "inv0", "A13", "G1",
+    "rot0", "G2", "inv1", "G5", "G3", "G4", "rot1", "inv2", "A14", "H1", "inv3", "H2", "H3",
+    "rot2", "H5", "A15", "H4", "G6", "G7", "rot3", "G8", "rotd", "G9", "G10", "G11", "G12",
+    "H7", "H6", "H9", "W0", "H8", "H11", "H12", "G13", "H10", "G14", "G15", "H13", "W1", "zG0",
+    "pG1", "H14", "W2", "W3", "H15", "W4", "W5", "zH0", "zG1", "pG2", "pH1", "W6", "W7", "W9",
+    "W8", "W11", "W12", "zH1", "pH2", "W10", "W13", "zG2", "pG3", "W14", "zH2", "pH3", "W15",
+    "zG3", "zH3", "zG4", "sc00", "sc01", "sc02", "zH4", "sc03", "sc10", "sc11", "qt", "sc12",
+    "sc13",
+)
 HALF = (LEN, LEN + RANK)
 
 
@@ -198,6 +222,7 @@
     left,
     qout_t,
     mixed,
+    weighted,
     tiles1,
     landed1,
     tiles2,
@@ -323,11 +348,7 @@
         def _():
             no()
 
-    for copy in loads[:3]:
-        copy.wait()
-    for h in range(2):
-        one_of(shifts, shift[h].start, shift_here[h].start)
-    for copy in loads[3:6]:
+    for copy in loads[:6]:
         copy.wait()
     gather_acts = Gather(place, acts_all, acts_send, acts_recv)
     gather_grads = [
@@ -335,19 +356,22 @@
         Gather(place, grads1, grads_send1, grads_recv1),
     ]
     gather_wide = Gather(place, wide_all, wide_send, wide_recv)
-    acts_queue = gather_acts.events()
-    grads_queue = [gather.events() for gather in gather_grads]
-    wide_queue = gather_wide.events()
-
-    def serve(queue, n):
-        for _ in range(n):
-            if queue:
-                queue.pop(0)()
-
-    serve(acts_queue, 1)
-    for h in range(2):
+    run = {}
+    for letter, gather, plan in (
+        ("A", gather_acts, PLAN_A),
+        ("G", gather_grads[0], PLAN_G),
+        ("H", gather_grads[1], PLAN_G),
+        ("W", gather_wide, PLAN_W),
+    ):
+        for index, event in enumerate(gather.events(plan)):
+            run[letter + str(index)] = event
+
+    def relay_block(h):
         one_of(shifts, shift[h].wait, shift_here[h].wait)
         one_of(moves, permute[h].start, permute_here[h].start)
+
+    def take_block(h):
+        one_of(moves, permute[h].wait, permute_here[h].wait)
 
     sum_first, sum_second, sum_last, sum1_sent = plane_sum(
         place, tiles1, landed1, sum1_send, sum1_recv
@@ -379,7 +403,7 @@
     def invert(start, stop):
         def body(slot, carry):
             columns = pl.ds(pl.multiple_of(slot * FEAT, FEAT), FEAT)
-            inverse[slot] = 1.0 / (eig_v[:, columns].astype(F32) + damping)
+            inverse[slot] = 1.0 / (eig_v[:, columns].astype(F32) + scale[0])
             return carry
 
         lax.fori_loop(start, stop, body, 0)
@@ -387,17 +411,25 @@
     qin_sent = []
     my_query = pl.ds(pl.multiple_of(TOKENS + z * RANK, RANK), RANK)
 
-    def rotate_in():
-        gather_acts.rest()
-        loads[8].wait()
-        acc_in[...] = jnp.zeros_like(acc_in)
-
-        def body(slot, carry):
+    def group_slots(group):
+        return [
+            slot_of(x, y, lax.rem(core + k, 2), GROUPS[group], k // 2) for k in range(2 * SIDE)
+        ]
+
+    def rotate_group(group):
+        gather_acts.group(GROUPS[group])
+        if group == 0:
+            loads[8].wait()
+            acc_in[...] = jnp.zeros_like(acc_in)
+
+        total = None
+        for slot in group_slots(group):
             rows = pl.ds(pl.multiple_of(slot * FEAT, FEAT), FEAT)
-            acc_in[...] += jnp.dot(acts_all[slot], bin_v[rows, :], preferred_element_type=F32)
-            return carry
-
-        lax.fori_loop(0, DEVICES, body, 0)
+            term = jnp.dot(acts_all[slot], bin_v[rows, :], preferred_element_type=F32)
+            total = term if total is None else total + term
+        acc_in[...] += total
+
+    def rotated():
         position = lax.broadcasted_iota(jnp.int32, (LEN, FEAT), 0)
         for s in range(2):
             rows = pl.ds(s * LEN, LEN)
@@ -452,115 +484,116 @@
         z_sent.append(copy)
         last[h, way] = copy
 
+    products = {}
+
+    def product(h, step):
+        products[h] = pair(h, ((4, -3), (3, -2), (2, -1), (1, 0))[step])
+
     def reduce_step(h, step):
         if step == 0:
-            a, b = pair(h, (4, -3))
+            gather_grads[h].rest()
+            product(h, 0)
+            a, b = products[h]
             kept_a[h][0] = a.astype(BF16)
             hop(h, 0, 0)
             kept_b[h][0] = b.astype(BF16)
             hop(h, 1, 0)
-        elif step < 3:
-            a, b = pair(h, (4 - step, step - 3))
+        elif step < 4:
+            a, b = products[h]
             last[h, 0].wait_recv()
             kept_a[h][step] = (a + landed_a[h][step - 1].astype(F32)).astype(BF16)
             hop(h, 0, step)
             last[h, 1].wait_recv()
-            kept_b[h][step] = (b + landed_b[h][step - 1].astype(F32)).astype(BF16)
-            hop(h, 1, step)
-        elif step == 3:
-            a, b = pair(h, (1, 0))
-            last[h, 0].wait_recv()
-            kept_a[h][3] = (a + landed_a[h][2].astype(F32)).astype(BF16)
-            hop(h, 0, 3)
-            last[h, 1].wait_recv()
-            mine[h][...] = b + landed_b[h][2].astype(F32)
+            b = b + landed_b[h][step - 1].astype(F32)
+            if step < 3:
+                kept_b[h][step] = b.astype(BF16)
+                hop(h, 1, step)
+            else:
+                mine[h][...] = b
         else:
             last[h, 0].wait_recv()
             mine[h][...] += landed_a[h][3].astype(F32)
             pad[pl.ds(0, LEN), pl.ds(0, HID)] = mine[h][pl.ds(0, LEN), :]
             left[h] = pad[...].T.astype(BF16)
-
-    pad[...] = jnp.zeros_like(pad)
-    serve(acts_queue, 5)
-    sum_eig()
-    serve(acts_queue, 4)
-    for h in range(2):
-        one_of(moves, permute[h].wait, permute_here[h].wait)
-        serve(grads_queue[h], 1)
-    serve(acts_queue, 6)
-    serve(grads_queue[0], 5)
-    sum_second()
-    turn_basis()
-    serve(grads_queue[0], 4)
-    rotate_in()
-    serve(grads_queue[0], 6)
-    serve(grads_queue[1], 5)
-    damping = 0.1 * jnp.sum(sum_last()) / (FF * D)
-    gather_grads[0].rest()
-    reduce_step(0, 0)
-    serve(grads_queue[1], 4)
-    invert(0, 8)
-    reduce_step(0, 1)
-    serve(grads_queue[1], 3)
-    for copy in qin_sent:
-        copy.wait_recv()
-    serve(wide_queue, 1)
-    serve(grads_queue[1], 3)
-    reduce_step(0, 2)
-    serve(wide_queue, 2)
-    gather_grads[1].rest()
-    reduce_step(1, 0)
-    serve(wide_queue, 3)
-    reduce_step(0, 3)
-    invert(8, 16)
-    reduce_step(1, 1)
-    serve(wide_queue, 3)
-    reduce_step(0, 4)
-    invert(16, 24)
-    reduce_step(1, 2)
-    serve(wide_queue, 4)
-    invert(24, 32)
-    reduce_step(1, 3)
-    serve(wide_queue, 3)
-    reduce_step(1, 4)
+            if h:
+                send_qout()
 
     my_rows = pl.ds(pl.multiple_of(z * RANK, RANK), RANK)
-    qout_all[my_rows, :] = mine1[pl.ds(LEN, RANK), :].astype(BF16)
     qout_sent = []
-    for o in range(1, PLANES):
-        copy = pltpu.make_async_remote_copy(
-            src_ref=qout_all.at[my_rows],
-            dst_ref=qout_all.at[my_rows],
-            send_sem=qout_send.at[o],
-            recv_sem=qout_recv.at[o],
-            device_id=(mod(z + o, PLANES), m),
-            device_id_type=MESH,
-        )
-        copy.start()
-        qout_sent.append(copy)
-
-    gather_wide.rest()
-    mixed[...] = jnp.zeros_like(mixed)
-
-    def score(slot, carry):
-        queries = wide_all[slot, pl.ds(TOKENS, QROWS), :]
-        for s in range(2):
+
+    def send_qout():
+        qout_all[my_rows, :] = mine1[pl.ds(LEN, RANK), :].astype(BF16)
+        for o in range(1, PLANES):
+            copy = pltpu.make_async_remote_copy(
+                src_ref=qout_all.at[my_rows],
+                dst_ref=qout_all.at[my_rows],
+                send_sem=qout_send.at[o],
+                recv_sem=qout_recv.at[o],
+                device_id=(mod(z + o, PLANES), m),
+                device_id_type=MESH,
+            )
+            copy.start()
+            qout_sent.append(copy)
+
+    arrived = set()
+
+    def score(s, group):
+        if group not in arrived:
+            arrived.add(group)
+            gather_wide.group(GROUPS[group])
+
+        slots = group_slots(group)
+        for k, slot in enumerate(slots):
             outer = jnp.dot(
                 left[s, pl.ds(0, HID), :],
                 wide_all[slot, pl.ds(s * LEN, 128), :],
                 preferred_element_type=F32,
             )
-            weighted = (outer * inverse[slot]).astype(BF16)
-            mixed[s] += lax.dot_general(
-                weighted, queries, (((1,), (1,)), ((), ())), preferred_element_type=F32
-            )
-        return carry
-
-    lax.fori_loop(0, DEVICES, score, 0)
-    for copy in qout_sent:
-        copy.wait_recv()
-    pad[:, pl.ds(0, HID)] = qout_all[...].astype(F32)
-    qout_t[...] = pad[...].T
+            weighted[:, pl.ds(k * FEAT, FEAT)] = (outer * inverse[slot]).astype(BF16)
+        queries = [wide_all[slot, pl.ds(TOKENS, QROWS), :] for slot in slots]
+        mixed[s] += lax.dot_general(
+            weighted[...],
+            jnp.concatenate(queries, axis=1),
+            (((1,), (1,)), ((), ())),
+            preferred_element_type=F32,
+        )
+
+    def turn_queries():
+        for copy in qout_sent:
+            copy.wait_recv()
+        pad[:, pl.ds(0, HID)] = qout_all[...].astype(F32)
+        qout_t[...] = pad[...].T
+
+    def start_wide():
+        for copy in qin_sent:
+            copy.wait_recv()
+        run["W"]()
+
+    scale = []
+
+    def damp():
+        scale.append(0.1 * jnp.sum(sum_last()) / (FF * D))
+
+    run["W"], run["W0"] = run["W0"], start_wide
+    for h, letter in enumerate("GH"):
+        run["s" + letter] = functools.partial(one_of, shifts, shift[h].start, shift_here[h].start)
+        run["r" + letter] = functools.partial(relay_block, h)
+        run["t" + letter] = functools.partial(take_block, h)
+        for step in range(5):
+            run["z" + letter + str(step)] = functools.partial(reduce_step, h, step)
+            run["p" + letter + str(step)] = functools.partial(product, h, step)
+    for group in range(SIDE):
+        run["rot" + str(group)] = functools.partial(rotate_group, group)
+        run["inv" + str(group)] = functools.partial(invert, 8 * group, 8 * group + 8)
+        for s in range(2):
+            run["sc" + str(s) + str(group)] = functools.partial(score, s, group)
+    run.update(eig=sum_eig, eig2=sum_second, turn=turn_basis, damp=damp, qt=turn_queries, rotd=rotated)
+
+    pad[...] = jnp.zeros_like(pad)
+    mixed[...] = jnp.zeros_like(mixed)
+    for name in SCHEDULE:
+        run[name]()
+
     tiles2[0] = jnp.zeros((8, 128), F32)
     for s in range(2):
         tiles2[0, pl.ds(s, 1), :] = jnp.sum(
@@ -618,6 +651,7 @@
             pltpu.VMEM((2, 512, 128), BF16),
             pltpu.VMEM((512, 128), F32),
             pltpu.VMEM((2, HID, QROWS), F32),
+            pltpu.VMEM((HID, 2 * SIDE * FEAT), BF16),
             pltpu.VMEM((2, 8, 128), F32),
             pltpu.VMEM((10, 8, 128), F32),
             pltpu.VMEM((2, 8, 128), F32),

time: 116 us -> 96.2 us (0.83)
  Pallas kernels: 115 us -> 94.7 us
    pallas_call x1, Pallas kernels: 115 us -> 94.7 us  [per_device(): pl.pallas_call(kernel, out_shape=jax.ShapeDtypeStruct((2, 128), F32), in_...]
where the time goes in v3:
time: 96.2 us
  Pallas kernels  94.7 us (98%)
    pallas_call x1, Pallas kernels, per_device(): pl.pallas_call(kernel, out_shape=jax.ShapeDtypeStruct((2, 128), F32), in_...  94.7 us

profile of v3, /device:TPU:1, one launch (start us, length us, event | category | flops | bytes accessed | tf_op | source)
XLA Modules:
  0.0 96.2 jit_solution(5948934047967496372)
XLA Ops:
  0.0 94.7 %shard_map.82 = f32[2,128]{1,0:T(2,128)} custom-call(bf16[2,96,256]{2,1,0:T(8,128)(2,1)} %acts.1, bf16[2,96,448]{2,1,0:T(8,128)(2,1)} %grads.1, s32[2]{0:T(128)} %counts.1, bf16[8192,256]{1,0:T(8,128)(2,1)} %basis_in.1, bf16[448,1792]{1,0:T(8,128)(2,1)} %bitcast.1, bf16[448,8192]{1,0:T(8,128)(2,1)} %eigvals.1, bf16[1,16,448]{2,1,0:T(8,128)(2,1)} %query_out.1, ...), custom_call_target="tpu_custom_call" | custom-call | tf_op jit(solution)/shard_map/pallas_call | solution.py:626
  94.7 0.8 reshape.3
  95.5 0.7 reduce_sum.9

commit v4 on v3

--- a/solution.py
+++ b/solution.py
@@ -170,17 +170,24 @@
 
 PLAN_A, PLAN_G, PLAN_W = RING, EARLY, RING
 SCHEDULE = (
-    "sG", "sH", "A0", "turn", "eig", "rG", "rH", "A1", "A2", "A3", "A4", "eig2", "A5", "A7",
-    "tG", "G0", "A6", "A9", "A8", "A12", "damp", "tH", "H0", "A11", "A10", "inv0", "A13", "G1",
-    "rot0", "G2", "inv1", "G5", "G3", "G4", "rot1", "inv2", "A14", "H1", "inv3", "H2", "H3",
-    "rot2", "H5", "A15", "H4", "G6", "G7", "rot3", "G8", "rotd", "G9", "G10", "G11", "G12",
-    "H7", "H6", "H9", "W0", "H8", "H11", "H12", "G13", "H10", "G14", "G15", "H13", "W1", "zG0",
-    "pG1", "H14", "W2", "W3", "H15", "W4", "W5", "zH0", "zG1", "pG2", "pH1", "W6", "W7", "W9",
-    "W8", "W11", "W12", "zH1", "pH2", "W10", "W13", "zG2", "pG3", "W14", "zH2", "pH3", "W15",
-    "zG3", "zH3", "zG4", "sc00", "sc01", "sc02", "zH4", "sc03", "sc10", "sc11", "qt", "sc12",
-    "sc13",
+    "sG", "sH", "sI", "sJ", "A0", "turn", "eig", "rG", "rH", "rI", "rJ", "A1", "A2", "A3",
+    "A4", "eig2", "tG", "G0", "A5", "tH", "H0", "A7", "A6", "A9", "tI", "I0", "G2", "A8", "G4",
+    "A12", "damp", "inv0", "G1", "H2", "G3", "G5", "A11", "H4", "tJ", "J0", "A10", "rot0",
+    "H1", "H5", "A13", "H3", "A14", "inv1", "I1", "I2", "I3", "I4", "I5", "G8", "G9", "G6",
+    "rot1", "G7", "H8", "H9", "G12", "G11", "rot2", "G10", "J2", "J1", "inv2", "J4", "J5",
+    "J3", "H7", "inv3", "H11", "A15", "I7", "H6", "I9", "H10", "I11", "H12", "G14", "I6",
+    "rot3", "G13", "H14", "I8", "rotd", "G15", "J7", "J9", "I10", "J8", "J11", "I12", "H13",
+    "J6", "zG0", "pG1", "J10", "J12", "I13", "I14", "H15", "W0", "J13", "I15", "J14", "zH0",
+    "pH1", "zG1", "pG2", "zI0", "pI1", "J15", "W1", "W2", "zH1", "pH2", "zJ0", "zG2", "pG3",
+    "pJ1", "zI1", "pI2", "W3", "W4", "W5", "W7", "zH2", "pH3", "W6", "W9", "zJ1", "pJ2", "W8",
+    "zG3", "zI2", "pI3", "W11", "W12", "zH3", "W13", "W10", "zJ2", "pJ3", "zG4", "W14", "zI3",
+    "zH4", "sc00", "sc01", "zJ3", "W15", "zI4", "sc02", "sc03", "zJ4", "sc10", "sc11", "sc12",
+    "qt", "sc13",
 )
-HALF = (LEN, LEN + RANK)
+PART = LEN // 2
+CHUNKS = (PART, PART, PART, PART + RANK)
+SUMMED = (PART, PART, PART, PART + 2 * RANK)
+LETTERS = "GHIJ"
 
 
 def kernel(
@@ -193,85 +200,25 @@
     query_out,
     query_in,
     out,
-    bin_v,
-    bout_t,
-    bout_v,
-    eig_v,
-    inverse,
-    acts_all,
-    stage0,
-    stage1,
-    relay0,
-    relay1,
-    grads0,
-    grads1,
-    wide_all,
-    acc_in,
-    send_a0,
-    send_b0,
-    got_a0,
-    got_b0,
-    send_a1,
-    send_b1,
-    got_a1,
-    got_b1,
-    mine0,
-    mine1,
-    qout_all,
-    pad,
-    left,
-    qout_t,
-    mixed,
-    weighted,
-    tiles1,
-    landed1,
-    tiles2,
-    landed2,
-    local_sems,
-    acts_send,
-    acts_recv,
-    grads_send0,
-    grads_recv0,
-    grads_send1,
-    grads_recv1,
-    wide_send,
-    wide_recv,
-    perm_sems,
-    qin_send,
-    qin_recv,
-    qout_send,
-    qout_recv,
-    z_send,
-    z_recv,
-    sum1_send,
-    sum1_recv,
-    sum2_send,
-    sum2_recv,
+    *scratch,
 ):
+    names = iter(scratch)
+    bin_v, bout_t, bout_v, eig_v, inverse, acts_all, wide_all, acc_in = (next(names) for _ in range(8))
+    qout_all, pad, left, qout_t, mixed, weighted = (next(names) for _ in range(6))
+    tiles1, landed1, tiles2, landed2 = (next(names) for _ in range(4))
+    stage, relay, grads_all, kept_a, kept_b, landed_a, landed_b, mine = (
+        [next(names) for _ in CHUNKS] for _ in range(8)
+    )
+    local_sems, perm_sems, qin_send, qin_recv, qout_send, qout_recv = (next(names) for _ in range(6))
+    z_send, z_recv, sum1_send, sum1_recv, sum2_send, sum2_recv = (next(names) for _ in range(6))
+    gather_sems = [(next(names), next(names)) for _ in range(6)]
+
     z = lax.axis_index("grp")
     m = lax.axis_index("mp")
     core = lax.rem(m, 2)
     chip = lax.div(m, 2)
     x, y = lax.div(chip, SIDE), lax.rem(chip, SIDE)
     place = (z, m, x, y, core)
-    stage, relay, grads_all = (stage0, stage1), (relay0, relay1), (grads0, grads1)
-
-    loads = []
-
-    def load(src, dst):
-        copy = pltpu.make_async_copy(src, dst, local_sems.at[len(loads)])
-        copy.start()
-        loads.append(copy)
-
-    load(grads.at[0], stage0)
-    load(grads.at[1], stage1.at[pl.ds(0, LEN)])
-    load(query_out.at[0], stage1.at[pl.ds(LEN, RANK)])
-    load(acts.at[0], acts_all.at[m, pl.ds(0, LEN)])
-    load(acts.at[1], acts_all.at[m, pl.ds(LEN, LEN)])
-    load(query_in.at[0], acts_all.at[m, pl.ds(TOKENS, RANK)])
-    load(eigvals, eig_v)
-    load(basis_out, bout_t.at[pl.ds(0, HID)])
-    load(basis_in, bin_v)
 
     y_low, y_high = lax.rem(y, 2), lax.div(y, 2)
 
@@ -308,35 +255,56 @@
             barrier, inc=1, device_id=(from_plane, from_device), device_id_type=MESH
         )
 
+    loads = []
+
+    def load(src, dst):
+        copy = pltpu.make_async_copy(src, dst, local_sems.at[len(loads)])
+        copy.start()
+        loads.append(copy)
+
+    for h in range(len(CHUNKS)):
+        rows = pl.ds(h % 2 * PART, PART)
+        load(grads.at[h // 2, rows], stage[h].at[pl.ds(0, PART)])
+    load(query_out.at[0], stage[-1].at[pl.ds(PART, RANK)])
+    load(acts.at[0], acts_all.at[m, pl.ds(0, LEN)])
+    load(acts.at[1], acts_all.at[m, pl.ds(LEN, LEN)])
+    load(query_in.at[0], acts_all.at[m, pl.ds(TOKENS, RANK)])
+    first_loads = list(loads)
+    load(eigvals, eig_v)
+    load(basis_out, bout_t.at[pl.ds(0, HID)])
+    load(basis_in, bin_v)
+    load_eig, load_out, load_in = loads[-3:]
+
     pl.semaphore_wait(
         barrier, len(row) + len(column) + PLANES - 1 + jnp.where(stays, 0, 1)
     )
 
     shift, shift_here, permute, permute_here = [], [], [], []
-    for h in range(2):
+    chunks = len(CHUNKS)
+    for h in range(chunks):
         shift.append(
             pltpu.make_async_remote_copy(
                 src_ref=stage[h],
                 dst_ref=relay[h],
-                send_sem=perm_sems.at[h],
-                recv_sem=perm_sems.at[2 + h],
+                send_sem=perm_sems.at[0, h],
+                recv_sem=perm_sems.at[1, h],
                 device_id=(z, relay_to),
                 device_id_type=MESH,
             )
         )
-        shift_here.append(pltpu.make_async_copy(stage[h], relay[h], perm_sems.at[4 + h]))
+        shift_here.append(pltpu.make_async_copy(stage[h], relay[h], perm_sems.at[2, h]))
         permute.append(
             pltpu.make_async_remote_copy(
                 src_ref=relay[h],
                 dst_ref=grads_all[h].at[to],
-                send_sem=perm_sems.at[6 + h],
-                recv_sem=perm_sems.at[8 + h],
+                send_sem=perm_sems.at[3, h],
+                recv_sem=perm_sems.at[4, h],
                 device_id=(plane, to),
                 device_id_type=MESH,
             )
         )
         permute_here.append(
-            pltpu.make_async_copy(relay[h], grads_all[h].at[m], perm_sems.at[10 + h])
+            pltpu.make_async_copy(relay[h], grads_all[h].at[m], perm_sems.at[5, h])
         )
 
     def one_of(predicate, yes, no):
@@ -348,20 +316,16 @@
         def _():
             no()
 
-    for copy in loads[:6]:
+    for copy in first_loads:
         copy.wait()
-    gather_acts = Gather(place, acts_all, acts_send, acts_recv)
-    gather_grads = [
-        Gather(place, grads0, grads_send0, grads_recv0),
-        Gather(place, grads1, grads_send1, grads_recv1),
-    ]
-    gather_wide = Gather(place, wide_all, wide_send, wide_recv)
+    gather_acts = Gather(place, acts_all, *gather_sems[0])
+    gather_wide = Gather(place, wide_all, *gather_sems[1])
+    gather_grads = [Gather(place, grads_all[h], *gather_sems[2 + h]) for h in range(chunks)]
     run = {}
     for letter, gather, plan in (
         ("A", gather_acts, PLAN_A),
-        ("G", gather_grads[0], PLAN_G),
-        ("H", gather_grads[1], PLAN_G),
         ("W", gather_wide, PLAN_W),
+        *((letter, gather, PLAN_G) for letter, gather in zip(LETTERS, gather_grads)),
     ):
         for index, event in enumerate(gather.events(plan)):
             run[letter + str(index)] = event
@@ -378,7 +342,7 @@
     )
 
     def sum_eig():
-        loads[6].wait()
+        load_eig.wait()
 
         def add_eig(slot, total):
             columns = pl.ds(pl.multiple_of(slot * FEAT, FEAT), FEAT)
@@ -390,7 +354,7 @@
         sum_first()
 
     def turn_basis():
-        loads[7].wait()
+        load_out.wait()
 
         def turn(i, carry):
             rows = pl.ds(pl.multiple_of(i * 128, 128), 128)
@@ -419,7 +383,7 @@
     def rotate_group(group):
         gather_acts.group(GROUPS[group])
         if group == 0:
-            loads[8].wait()
+            load_in.wait()
             acc_in[...] = jnp.zeros_like(acc_in)
 
         total = None
@@ -451,9 +415,6 @@
     toward = 1 - 2 * core
     ahead = mod(z + toward, PLANES)
     behind = mod(z - toward, PLANES)
-    kept_a, kept_b = (send_a0, send_a1), (send_b0, send_b1)
-    landed_a, landed_b = (got_a0, got_a1), (got_b0, got_b1)
-    mine = (mine0, mine1)
     z_sent = []
     last = {}
 
@@ -468,7 +429,7 @@
                 preferred_element_type=F32,
             )
             total = term if total is None else total + term
-        return total[: HALF[h]], total[HALF[h] :]
+        return total[: CHUNKS[h]], total[CHUNKS[h] :]
 
     def hop(h, way, step):
         index = h * 7 + way * 4 + step
@@ -485,44 +446,63 @@
         last[h, way] = copy
 
     products = {}
+    turned = set()
 
     def product(h, step):
         products[h] = pair(h, ((4, -3), (3, -2), (2, -1), (1, 0))[step])
+
+    def keep(ref, step, value):
+        tokens = value[:PART].astype(BF16)
+        ref[step, pl.ds(0, PART), :] = tokens
+        if value.shape[0] > PART:
+            high = value[PART:].astype(BF16)
+            ref[step, pl.ds(PART, RANK), :] = high
+            ref[step, pl.ds(PART + RANK, RANK), :] = (value[PART:] - high.astype(F32)).astype(BF16)
+
+    def landed(ref, step):
+        value = ref[step].astype(F32)
+        if value.shape[0] == PART:
+            return value
+        query = value[PART : PART + RANK] + value[PART + RANK :]
+        return jnp.concatenate([value[:PART], query], axis=0)
 
     def reduce_step(h, step):
         if step == 0:
             gather_grads[h].rest()
             product(h, 0)
             a, b = products[h]
-            kept_a[h][0] = a.astype(BF16)
+            keep(kept_a[h], 0, a)
             hop(h, 0, 0)
-            kept_b[h][0] = b.astype(BF16)
+            keep(kept_b[h], 0, b)
             hop(h, 1, 0)
         elif step < 4:
             a, b = products[h]
             last[h, 0].wait_recv()
-            kept_a[h][step] = (a + landed_a[h][step - 1].astype(F32)).astype(BF16)
+            keep(kept_a[h], step, a + landed(landed_a[h], step - 1))
             hop(h, 0, step)
             last[h, 1].wait_recv()
-            b = b + landed_b[h][step - 1].astype(F32)
+            b = b + landed(landed_b[h], step - 1)
             if step < 3:
-                kept_b[h][step] = b.astype(BF16)
+                keep(kept_b[h], step, b)
                 hop(h, 1, step)
             else:
                 mine[h][...] = b
         else:
             last[h, 0].wait_recv()
-            mine[h][...] += landed_a[h][3].astype(F32)
-            pad[pl.ds(0, LEN), pl.ds(0, HID)] = mine[h][pl.ds(0, LEN), :]
-            left[h] = pad[...].T.astype(BF16)
-            if h:
-                send_qout()
+            value = mine[h][...] + landed(landed_a[h], 3)
+            s = h // 2
+            pad[s, pl.ds(h % 2 * PART, PART), pl.ds(0, HID)] = value[:PART]
+            if s in turned:
+                left[s] = pad[s].T.astype(BF16)
+            turned.add(s)
+            if h == chunks - 1:
+                send_qout(value[PART:])
 
     my_rows = pl.ds(pl.multiple_of(z * RANK, RANK), RANK)
     qout_sent = []
 
-    def send_qout():
-        qout_all[my_rows, :] = mine1[pl.ds(LEN, RANK), :].astype(BF16)
+    def send_qout(rotated_query):
+        qout_all[my_rows, :] = rotated_query.astype(BF16)
         for o in range(1, PLANES):
             copy = pltpu.make_async_remote_copy(
                 src_ref=qout_all.at[my_rows],
@@ -561,8 +541,8 @@
     def turn_queries():
         for copy in qout_sent:
             copy.wait_recv()
-        pad[:, pl.ds(0, HID)] = qout_all[...].astype(F32)
-        qout_t[...] = pad[...].T
+        pad[2, :, pl.ds(0, HID)] = qout_all[...].astype(F32)
+        qout_t[...] = pad[2].T
 
     def start_wide():
         for copy in qin_sent:
@@ -575,7 +555,7 @@
         scale.append(0.1 * jnp.sum(sum_last()) / (FF * D))
 
     run["W"], run["W0"] = run["W0"], start_wide
-    for h, letter in enumerate("GH"):
+    for h, letter in enumerate(LETTERS):
         run["s" + letter] = functools.partial(one_of, shifts, shift[h].start, shift_here[h].start)
         run["r" + letter] = functools.partial(relay_block, h)
         run["t" + letter] = functools.partial(take_block, h)
@@ -617,58 +597,42 @@
 ):
     anywhere = pl.BlockSpec(memory_space=pl.ANY)
     dma = pltpu.SemaphoreType.DMA
-    halves = [
-        pltpu.VMEM((count, rows, HID), BF16)
-        for rows in HALF
-        for count in (4, 3, 4, 3)
-    ]
-    gather_sems = [dma((31,)), dma((32,))]
+    vmem = pltpu.VMEM
+    per_chunk = [[vmem((rows, HID), BF16) for rows in CHUNKS]] * 2
+    per_chunk.append([vmem((DEVICES, rows, HID), BF16) for rows in CHUNKS])
+    per_chunk += [[vmem((steps, rows, HID), BF16) for rows in SUMMED] for steps in (4, 3, 4, 3)]
+    per_chunk.append([vmem((rows, HID), F32) for rows in CHUNKS])
     summed = pl.pallas_call(
         kernel,
         out_shape=jax.ShapeDtypeStruct((2, 128), F32),
         in_specs=[anywhere, anywhere, pl.BlockSpec(memory_space=pltpu.SMEM)] + [anywhere] * 5,
         out_specs=pl.BlockSpec(memory_space=pltpu.VMEM),
         scratch_shapes=[
-            pltpu.VMEM((D, FEAT), BF16),
-            pltpu.VMEM((512, 4 * HID), BF16),
-            pltpu.VMEM((4 * HID, HID), BF16),
-            pltpu.VMEM((HID, D), BF16),
-            pltpu.VMEM((DEVICES, HID, FEAT), F32),
-            pltpu.VMEM((DEVICES, ROWS, FEAT), BF16),
-            pltpu.VMEM((HALF[0], HID), BF16),
-            pltpu.VMEM((HALF[1], HID), BF16),
-            pltpu.VMEM((HALF[0], HID), BF16),
-            pltpu.VMEM((HALF[1], HID), BF16),
-            pltpu.VMEM((DEVICES, HALF[0], HID), BF16),
-            pltpu.VMEM((DEVICES, HALF[1], HID), BF16),
-            pltpu.VMEM((DEVICES, WIDE, FEAT), BF16),
-            pltpu.VMEM((ROWS, FEAT), F32),
-            *halves,
-            pltpu.VMEM((HALF[0], HID), F32),
-            pltpu.VMEM((HALF[1], HID), F32),
-            pltpu.VMEM((QROWS, HID), BF16),
-            pltpu.VMEM((128, 512), F32),
-            pltpu.VMEM((2, 512, 128), BF16),
-            pltpu.VMEM((512, 128), F32),
-            pltpu.VMEM((2, HID, QROWS), F32),
-            pltpu.VMEM((HID, 2 * SIDE * FEAT), BF16),
-            pltpu.VMEM((2, 8, 128), F32),
-            pltpu.VMEM((10, 8, 128), F32),
-            pltpu.VMEM((2, 8, 128), F32),
-            pltpu.VMEM((10, 8, 128), F32),
-            dma((9,)),
-            *gather_sems * 4,
-            dma((12,)),
-            dma((8,)),
-            dma((8,)),
-            dma((8,)),
-            dma((8,)),
-            dma((14,)),
-            dma((14,)),
-            dma((10,)),
-            dma((10,)),
-            dma((10,)),
-            dma((10,)),
+            vmem((D, FEAT), BF16),
+            vmem((512, 4 * HID), BF16),
+            vmem((4 * HID, HID), BF16),
+            vmem((HID, D), BF16),
+            vmem((DEVICES, HID, FEAT), F32),
+            vmem((DEVICES, ROWS, FEAT), BF16),
+            vmem((DEVICES, WIDE, FEAT), BF16),
+            vmem((ROWS, FEAT), F32),
+            vmem((QROWS, HID), BF16),
+            vmem((3, 128, 512), F32),
+            vmem((2, 512, 128), BF16),
+            vmem((512, 128), F32),
+            vmem((2, HID, QROWS), F32),
+            vmem((HID, 2 * SIDE * FEAT), BF16),
+            vmem((2, 8, 128), F32),
+            vmem((10, 8, 128), F32),
+            vmem((2, 8, 128), F32),
+            vmem((10, 8, 128), F32),
+            *sum(per_chunk, []),
+            dma((11,)),
+            dma((6, len(CHUNKS))),
+            *[dma((PLANES,))] * 4,
+            *[dma((7 * len(CHUNKS),))] * 2,
+            *[dma((10,))] * 4,
+            *[dma((31,)), dma((32,))] * (2 + len(CHUNKS)),
         ],
         compiler_params=pltpu.CompilerParams(
             collective_id=0, has_side_effects=True, vmem_limit_bytes=60 * 1024 * 1024

time: 96.2 us -> 93.4 us (0.971)
  Pallas kernels: 94.7 us -> 91.9 us
    pallas_call x1, Pallas kernels: 94.7 us -> 91.9 us  [per_device(): pl.pallas_call(kernel, out_shape=jax.ShapeDtypeStruct((2, 128), F32), in_...]
where the time goes in v4:
time: 93.4 us; the launch traced here: 93.3 us
  Pallas kernels  91.9 us (98%)
    pallas_call x1, Pallas kernels, per_device(): pl.pallas_call(kernel, out_shape=jax.ShapeDtypeStruct((2, 128), F32), in_...  91.9 us

profile of v4, /device:TPU:1, one launch (start us, length us, event | category | flops | bytes accessed | tf_op | source)
XLA Modules:
  0.0 93.3 jit_solution(14463585414019025171)
XLA Ops:
  0.0 91.9 %shard_map.82 = f32[2,128]{1,0:T(2,128)} custom-call(bf16[2,96,256]{2,1,0:T(8,128)(2,1)} %acts.1, bf16[2,96,448]{2,1,0:T(8,128)(2,1)} %grads.1, s32[2]{0:T(128)} %counts.1, bf16[8192,256]{1,0:T(8,128)(2,1)} %basis_in.1, bf16[448,1792]{1,0:T(8,128)(2,1)} %bitcast.1, bf16[448,8192]{1,0:T(8,128)(2,1)} %eigvals.1, bf16[1,16,448]{2,1,0:T(8,128)(2,1)} %query_out.1, ...), custom_call_target="tpu_custom_call" | custom-call | tf_op jit(solution)/shard_map/pallas_call | solution.py:605
  91.9 0.8 reshape.3
  92.7 0.7 reduce_sum.9

commit v5 on v4

--- a/solution.py
+++ b/solution.py
@@ -50,6 +50,9 @@
     ((2, 2), (), ()),
 )
 EARLY = (((0, 0), (1, -1, 2), BOTH), ((-1, 0), (), BOTH)) + RING[2:]
+ALL = (1, -1, 2)
+DIRECT = (((0, 0), ALL, ALL),) + tuple(((d1, 0), (), ALL) for d1 in (-1, 1, 2))
+DIRECT += tuple(((d1, d2), (), ()) for d1 in (0, -1, 1, 2) for d2 in (-1, 1, 2))
 GROUPS = (0, -1, 1, 2)
 
 
@@ -168,26 +171,60 @@
     return row, column
 
 
-PLAN_A, PLAN_G, PLAN_W = RING, EARLY, RING
+PLAN_A, PLAN_G, PLAN_W = EARLY, EARLY, RING
 SCHEDULE = (
-    "sG", "sH", "sI", "sJ", "A0", "turn", "eig", "rG", "rH", "rI", "rJ", "A1", "A2", "A3",
-    "A4", "eig2", "tG", "G0", "A5", "tH", "H0", "A7", "A6", "A9", "tI", "I0", "G2", "A8", "G4",
-    "A12", "damp", "inv0", "G1", "H2", "G3", "G5", "A11", "H4", "tJ", "J0", "A10", "rot0",
-    "H1", "H5", "A13", "H3", "A14", "inv1", "I1", "I2", "I3", "I4", "I5", "G8", "G9", "G6",
-    "rot1", "G7", "H8", "H9", "G12", "G11", "rot2", "G10", "J2", "J1", "inv2", "J4", "J5",
-    "J3", "H7", "inv3", "H11", "A15", "I7", "H6", "I9", "H10", "I11", "H12", "G14", "I6",
-    "rot3", "G13", "H14", "I8", "rotd", "G15", "J7", "J9", "I10", "J8", "J11", "I12", "H13",
-    "J6", "zG0", "pG1", "J10", "J12", "I13", "I14", "H15", "W0", "J13", "I15", "J14", "zH0",
-    "pH1", "zG1", "pG2", "zI0", "pI1", "J15", "W1", "W2", "zH1", "pH2", "zJ0", "zG2", "pG3",
-    "pJ1", "zI1", "pI2", "W3", "W4", "W5", "W7", "zH2", "pH3", "W6", "W9", "zJ1", "pJ2", "W8",
-    "zG3", "zI2", "pI3", "W11", "W12", "zH3", "W13", "W10", "zJ2", "pJ3", "zG4", "W14", "zI3",
-    "zH4", "sc00", "sc01", "zJ3", "W15", "zI4", "sc02", "sc03", "zJ4", "sc10", "sc11", "sc12",
-    "qt", "sc13",
+    "sG", "sH", "sI", "sJ", "A0", "turn", "eig", "rG", "rH", "rI", "rJ", "A1", "A2", "A5",
+    "A3", "A4", "eig2", "tG", "G0", "A6", "A7", "A8", "A9", "tI", "I0", "A10", "A11", "G2",
+    "A12", "damp", "inv0", "G1", "G4", "G5", "rot0", "G3", "A13", "tH", "H0", "I1", "inv1",
+    "A14", "I2", "I3", "I5", "tJ", "J0", "A15", "I4", "rot1", "G8", "G9", "rot2", "G6", "G7",
+    "rot3", "G10", "G11", "H2", "G12", "rotd", "H1", "H3", "H4", "H5", "I6", "I7", "I8", "I9",
+    "I11", "I12", "J2", "I10", "J1", "G14", "J4", "J3", "J5", "G13", "H9", "G15", "H7", "H8",
+    "H11", "H6", "inv2", "H10", "H12", "zG0", "pG1", "I13", "I14", "H14", "H13", "I15", "J6",
+    "J7", "J8", "J9", "J10", "J11", "H15", "W0", "zI0", "pI1", "zH0", "pH1", "zG1", "pG2",
+    "J12", "J13", "J14", "J15", "inv3", "W1", "W2", "zI1", "pI2", "zH1", "pH2", "zJ0", "pJ1",
+    "W3", "W4", "zG2", "pG3", "W5", "zI2", "pI3", "zH2", "pH3", "zJ1", "pJ2", "W6", "W7", "W9",
+    "zG3", "W8", "zI3", "W11", "W12", "zH3", "zJ2", "pJ3", "W13", "W10", "zG4", "zI4", "W14",
+    "zH4", "sc00", "zJ3", "sc01", "qt", "W15", "sc02", "zJ4", "sc10", "sc03", "sc11", "sc12",
+    "sc13",
 )
-PART = LEN // 2
-CHUNKS = (PART, PART, PART, PART + RANK)
-SUMMED = (PART, PART, PART, PART + 2 * RANK)
+PARTS = ((0, 0, 64), (0, 64, 32), (1, 0, 64), (1, 64, 32))
+CHUNKS = tuple(rows + RANK * (h == 0) for h, (_, _, rows) in enumerate(PARTS))
+PACKED = tuple(rows * 7 // 2 + 4 * RANK * (h == 0) for h, (_, _, rows) in enumerate(PARTS))
+SUMMED = tuple(rows * 7 // 2 + 8 * RANK * (h == 0) for h, (_, _, rows) in enumerate(PARTS))
+HALF_LANES = 64
 LETTERS = "GHIJ"
+
+
+def pack(ref, rows, value, at=()):
+    value = value.astype(F32)
+    for t in range(3):
+        ref[(*at, pl.ds(t * rows, rows), slice(None))] = value[:, t * 128 : t * 128 + 128].astype(BF16)
+    half = rows // 2
+    first, second = value[:half, 384:], value[half:, 384:]
+    lane = lax.broadcasted_iota(jnp.int32, (half, 128), 1)
+    folded = jnp.where(lane < HALF_LANES, first, pltpu.roll(second, HALF_LANES, 1))
+    ref[(*at, pl.ds(3 * rows, half), slice(None))] = folded.astype(BF16)
+
+
+def unpack(value, rows, kind):
+    tiles = [value[t * rows : t * rows + rows].astype(kind) for t in range(3)]
+    folded = value[3 * rows : 3 * rows + rows // 2].astype(F32)
+    last = jnp.concatenate([folded, pltpu.roll(folded, HALF_LANES, 1)], axis=0)
+    return jnp.concatenate([*tiles, last.astype(kind)], axis=1)
+
+
+def pack_query(ref, start, value, at=()):
+    lane = lax.broadcasted_iota(jnp.int32, (RANK, 128), 1)
+    for t in range(4):
+        tile = value[:, t * 128 : t * 128 + 128].astype(F32)
+        if t == 3:
+            tile = jnp.where(lane < HALF_LANES, tile, 0.0)
+        ref[(*at, pl.ds(start + t * RANK, RANK), slice(None))] = tile.astype(BF16)
+
+
+def unpack_query(value, start, kind):
+    tiles = [value[start + t * RANK : start + t * RANK + RANK] for t in range(4)]
+    return jnp.concatenate(tiles, axis=1).astype(kind)
 
 
 def kernel(
@@ -206,8 +243,8 @@
     bin_v, bout_t, bout_v, eig_v, inverse, acts_all, wide_all, acc_in = (next(names) for _ in range(8))
     qout_all, pad, left, qout_t, mixed, weighted = (next(names) for _ in range(6))
     tiles1, landed1, tiles2, landed2 = (next(names) for _ in range(4))
-    stage, relay, grads_all, kept_a, kept_b, landed_a, landed_b, mine = (
-        [next(names) for _ in CHUNKS] for _ in range(8)
+    raw, stage, relay, grads_all, kept_a, kept_b, landed_a, landed_b, mine = (
+        [next(names) for _ in CHUNKS] for _ in range(9)
     )
     local_sems, perm_sems, qin_send, qin_recv, qout_send, qout_recv = (next(names) for _ in range(6))
     z_send, z_recv, sum1_send, sum1_recv, sum2_send, sum2_recv = (next(names) for _ in range(6))
@@ -262,10 +299,9 @@
         copy.start()
         loads.append(copy)
 
-    for h in range(len(CHUNKS)):
-        rows = pl.ds(h % 2 * PART, PART)
-        load(grads.at[h // 2, rows], stage[h].at[pl.ds(0, PART)])
-    load(query_out.at[0], stage[-1].at[pl.ds(PART, RANK)])
+    for h, (s, first, rows) in enumerate(PARTS):
+        load(grads.at[s, pl.ds(first, rows)], raw[h].at[pl.ds(0, rows)])
+    load(query_out.at[0], raw[0].at[pl.ds(PARTS[0][2], RANK)])
     load(acts.at[0], acts_all.at[m, pl.ds(0, LEN)])
     load(acts.at[1], acts_all.at[m, pl.ds(LEN, LEN)])
     load(query_in.at[0], acts_all.at[m, pl.ds(TOKENS, RANK)])
@@ -316,8 +352,15 @@
         def _():
             no()
 
+    pad[...] = jnp.zeros_like(pad)
     for copy in first_loads:
         copy.wait()
+    for h, (_, _, rows) in enumerate(PARTS):
+        pad[2, pl.ds(0, CHUNKS[h]), pl.ds(0, HID)] = raw[h][...].astype(F32)
+        value = pad[2, pl.ds(0, CHUNKS[h]), :]
+        pack(stage[h], rows, value[:rows])
+        if h == 0:
+            pack_query(stage[h], rows * 7 // 2, value[rows:])
     gather_acts = Gather(place, acts_all, *gather_sems[0])
     gather_wide = Gather(place, wide_all, *gather_sems[1])
     gather_grads = [Gather(place, grads_all[h], *gather_sems[2 + h]) for h in range(chunks)]
@@ -356,13 +399,21 @@
     def turn_basis():
         load_out.wait()
 
+        bout_t[pl.ds(HID, 512 - HID), :] = jnp.zeros((512 - HID, 4 * HID), BF16)
+
         def turn(i, carry):
-            rows = pl.ds(pl.multiple_of(i * 128, 128), 128)
-            turned = bout_t[:, rows].astype(F32).T
-            bout_v[rows, :] = turned[:, :HID].astype(BF16)
+            turned = bout_t[:, pl.ds(pl.multiple_of(i * 128, 128), 128)].astype(F32).T.astype(BF16)
+            for k in range(2):
+                piece = 2 * i + k
+                row = lax.div(piece, 7) * 512 + lax.rem(piece, 7) * HALF_LANES
+                rows = pl.ds(pl.multiple_of(row, HALF_LANES), HALF_LANES)
+                bout_v[rows, :] = turned[k * HALF_LANES : (k + 1) * HALF_LANES]
             return carry
 
         lax.fori_loop(0, 4 * HID // 128, turn, 0)
+        for j in range(4):
+            rows = pl.ds(j * 512 + HID, 512 - HID)
+            bout_v[rows, :] = jnp.zeros((512 - HID, 512), BF16)
 
     def invert(start, stop):
         def body(slot, carry):
@@ -422,10 +473,15 @@
         total = None
         slots = [mod(z + toward * offset, PLANES) for offset in offsets]
         for j in range(4):
-            lhs = [grads_all[h][place_of(z, j // 2, j % 2, source)] for source in slots]
+            lhs = []
+            for source in slots:
+                block = grads_all[h][place_of(z, j // 2, j % 2, source)]
+                lhs.append(unpack(block, PARTS[h][2], BF16))
+                if h == 0:
+                    lhs.append(unpack_query(block, PARTS[h][2] * 7 // 2, BF16))
             term = jnp.dot(
                 jnp.concatenate(lhs, axis=0),
-                bout_v[pl.ds(j * HID, HID), :],
+                bout_v[pl.ds(j * 512, 512), :],
                 preferred_element_type=F32,
             )
             total = term if total is None else total + term
@@ -451,58 +507,62 @@
     def product(h, step):
         products[h] = pair(h, ((4, -3), (3, -2), (2, -1), (1, 0))[step])
 
-    def keep(ref, step, value):
-        tokens = value[:PART].astype(BF16)
-        ref[step, pl.ds(0, PART), :] = tokens
-        if value.shape[0] > PART:
-            high = value[PART:].astype(BF16)
-            ref[step, pl.ds(PART, RANK), :] = high
-            ref[step, pl.ds(PART + RANK, RANK), :] = (value[PART:] - high.astype(F32)).astype(BF16)
-
-    def landed(ref, step):
-        value = ref[step].astype(F32)
-        if value.shape[0] == PART:
-            return value
-        query = value[PART : PART + RANK] + value[PART + RANK :]
-        return jnp.concatenate([value[:PART], query], axis=0)
+    def keep(h, ref, step, value):
+        rows = PARTS[h][2]
+        pack(ref, rows, value[:rows], (step,))
+        if h == 0:
+            query = value[rows:]
+            high = query.astype(BF16).astype(F32)
+            pack_query(ref, rows * 7 // 2, high, (step,))
+            pack_query(ref, rows * 7 // 2 + 4 * RANK, query - high, (step,))
+
+    def landed(h, ref, step):
+        rows = PARTS[h][2]
+        value = ref[step]
+        tokens = unpack(value, rows, F32)
+        if h:
+            return tokens
+        query = unpack_query(value, rows * 7 // 2, F32)
+        query = query + unpack_query(value, rows * 7 // 2 + 4 * RANK, F32)
+        return jnp.concatenate([tokens, query], axis=0)
 
     def reduce_step(h, step):
         if step == 0:
             gather_grads[h].rest()
             product(h, 0)
             a, b = products[h]
-            keep(kept_a[h], 0, a)
+            keep(h, kept_a[h], 0, a)
             hop(h, 0, 0)
-            keep(kept_b[h], 0, b)
+            keep(h, kept_b[h], 0, b)
             hop(h, 1, 0)
         elif step < 4:
             a, b = products[h]
             last[h, 0].wait_recv()
-            keep(kept_a[h], step, a + landed(landed_a[h], step - 1))
+            keep(h, kept_a[h], step, a + landed(h, landed_a[h], step - 1))
             hop(h, 0, step)
             last[h, 1].wait_recv()
-            b = b + landed(landed_b[h], step - 1)
+            b = b + landed(h, landed_b[h], step - 1)
             if step < 3:
-                keep(kept_b[h], step, b)
+                keep(h, kept_b[h], step, b)
                 hop(h, 1, step)
             else:
                 mine[h][...] = b
         else:
             last[h, 0].wait_recv()
-            value = mine[h][...] + landed(landed_a[h], 3)
-            s = h // 2
-            pad[s, pl.ds(h % 2 * PART, PART), pl.ds(0, HID)] = value[:PART]
+            value = mine[h][...] + landed(h, landed_a[h], 3)
+            s, first, rows = PARTS[h]
+            pad[s, pl.ds(first, rows), :] = value[:rows]
             if s in turned:
                 left[s] = pad[s].T.astype(BF16)
             turned.add(s)
-            if h == chunks - 1:
-                send_qout(value[PART:])
+            if h == 0:
+                send_qout(value[rows:])
 
     my_rows = pl.ds(pl.multiple_of(z * RANK, RANK), RANK)
     qout_sent = []
 
     def send_qout(rotated_query):
-        qout_all[my_rows, :] = rotated_query.astype(BF16)
+        qout_all[my_rows, :] = rotated_query[:, :HID].astype(BF16)
         for o in range(1, PLANES):
             copy = pltpu.make_async_remote_copy(
                 src_ref=qout_all.at[my_rows],
@@ -569,7 +629,6 @@
             run["sc" + str(s) + str(group)] = functools.partial(score, s, group)
     run.update(eig=sum_eig, eig2=sum_second, turn=turn_basis, damp=damp, qt=turn_queries, rotd=rotated)
 
-    pad[...] = jnp.zeros_like(pad)
     mixed[...] = jnp.zeros_like(mixed)
     for name in SCHEDULE:
         run[name]()
@@ -598,10 +657,11 @@
     anywhere = pl.BlockSpec(memory_space=pl.ANY)
     dma = pltpu.SemaphoreType.DMA
     vmem = pltpu.VMEM
-    per_chunk = [[vmem((rows, HID), BF16) for rows in CHUNKS]] * 2
-    per_chunk.append([vmem((DEVICES, rows, HID), BF16) for rows in CHUNKS])
-    per_chunk += [[vmem((steps, rows, HID), BF16) for rows in SUMMED] for steps in (4, 3, 4, 3)]
-    per_chunk.append([vmem((rows, HID), F32) for rows in CHUNKS])
+    per_chunk = [[vmem((rows, HID), BF16) for rows in CHUNKS]]
+    per_chunk += [[vmem((rows, 128), BF16) for rows in PACKED]] * 2
+    per_chunk.append([vmem((DEVICES, rows, 128), BF16) for rows in PACKED])
+    per_chunk += [[vmem((steps, rows, 128), BF16) for rows in SUMMED] for steps in (4, 3, 4, 3)]
+    per_chunk.append([vmem((rows, 512), F32) for rows in CHUNKS])
     summed = pl.pallas_call(
         kernel,
         out_shape=jax.ShapeDtypeStruct((2, 128), F32),
@@ -610,7 +670,7 @@
         scratch_shapes=[
             vmem((D, FEAT), BF16),
             vmem((512, 4 * HID), BF16),
-            vmem((4 * HID, HID), BF16),
+            vmem((4 * 512, 512), BF16),
             vmem((HID, D), BF16),
             vmem((DEVICES, HID, FEAT), F32),
             vmem((DEVICES, ROWS, FEAT), BF16),

time: 93.4 us -> 90.9 us (0.973)
  Pallas kernels: 91.9 us -> 89.4 us
    pallas_call x1, Pallas kernels: 91.9 us -> 89.4 us  [per_device(): pl.pallas_call(kernel, out_shape=jax.ShapeDtypeStruct((2, 128), F32), in_...]
where the time goes in v5:
time: 90.9 us
  Pallas kernels  89.4 us (98%)
    pallas_call x1, Pallas kernels, per_device(): pl.pallas_call(kernel, out_shape=jax.ShapeDtypeStruct((2, 128), F32), in_...  89.4 us

profile of v5, /device:TPU:1, one launch (start us, length us, event | category | flops | bytes accessed | tf_op | source)
XLA Modules:
  0.0 90.9 jit_solution(17860882430676119761)
XLA Ops:
  0.0 89.4 %shard_map.82 = f32[2,128]{1,0:T(2,128)} custom-call(bf16[2,96,256]{2,1,0:T(8,128)(2,1)} %acts.1, bf16[2,96,448]{2,1,0:T(8,128)(2,1)} %grads.1, s32[2]{0:T(128)} %counts.1, bf16[8192,256]{1,0:T(8,128)(2,1)} %basis_in.1, bf16[448,1792]{1,0:T(8,128)(2,1)} %bitcast.1, bf16[448,8192]{1,0:T(8,128)(2,1)} %eigvals.1, bf16[1,16,448]{2,1,0:T(8,128)(2,1)} %query_out.1, ...), custom_call_target="tpu_custom_call" | custom-call | tf_op jit(solution)/shard_map/pallas_call | solution.py:665
  89.4 0.8 reshape.3
  90.2 0.7 reduce_sum.9

commit v6 on v5

--- a/solution.py
+++ b/solution.py
@@ -173,7 +173,7 @@
 
 PLAN_A, PLAN_G, PLAN_W = EARLY, EARLY, RING
 SCHEDULE = (
-    "sG", "sH", "sI", "sJ", "A0", "turn", "eig", "rG", "rH", "rI", "rJ", "A1", "A2", "A5",
+    "sG", "sH", "sI", "sJ", "A0", "eig", "rG", "rH", "rI", "rJ", "turn", "A1", "A2", "A5",
     "A3", "A4", "eig2", "tG", "G0", "A6", "A7", "A8", "A9", "tI", "I0", "A10", "A11", "G2",
     "A12", "damp", "inv0", "G1", "G4", "G5", "rot0", "G3", "A13", "tH", "H0", "I1", "inv1",
     "A14", "I2", "I3", "I5", "tJ", "J0", "A15", "I4", "rot1", "G8", "G9", "rot2", "G6", "G7",
@@ -353,14 +353,24 @@
             no()
 
     pad[...] = jnp.zeros_like(pad)
-    for copy in first_loads:
-        copy.wait()
-    for h, (_, _, rows) in enumerate(PARTS):
+
+    def shift_block(h):
+        first_loads[h].wait()
+        if h == 0:
+            first_loads[chunks].wait()
         pad[2, pl.ds(0, CHUNKS[h]), pl.ds(0, HID)] = raw[h][...].astype(F32)
         value = pad[2, pl.ds(0, CHUNKS[h]), :]
+        rows = PARTS[h][2]
         pack(stage[h], rows, value[:rows])
         if h == 0:
             pack_query(stage[h], rows * 7 // 2, value[rows:])
+        one_of(shifts, shift[h].start, shift_here[h].start)
+
+    def start_acts():
+        for copy in first_loads[chunks + 1 :]:
+            copy.wait()
+        run["A"]()
+
     gather_acts = Gather(place, acts_all, *gather_sems[0])
     gather_wide = Gather(place, wide_all, *gather_sems[1])
     gather_grads = [Gather(place, grads_all[h], *gather_sems[2 + h]) for h in range(chunks)]
@@ -615,8 +625,9 @@
         scale.append(0.1 * jnp.sum(sum_last()) / (FF * D))
 
     run["W"], run["W0"] = run["W0"], start_wide
+    run["A"], run["A0"] = run["A0"], start_acts
     for h, letter in enumerate(LETTERS):
-        run["s" + letter] = functools.partial(one_of, shifts, shift[h].start, shift_here[h].start)
+        run["s" + letter] = functools.partial(shift_block, h)
         run["r" + letter] = functools.partial(relay_block, h)
         run["t" + letter] = functools.partial(take_block, h)
         for step in range(5):

time: 90.9 us -> 90.5 us (level)
  no operation moved by 1% of the time
where the time goes in v6:
time: 90.5 us; the launch traced here: 90.4 us
  Pallas kernels  89 us (98%)
    pallas_call x1, Pallas kernels, per_device(): pl.pallas_call(kernel, out_shape=jax.ShapeDtypeStruct((2, 128), F32), in_...  89 us

profile of v6, /device:TPU:1, one launch (start us, length us, event | category | flops | bytes accessed | tf_op | source)
XLA Modules:
  0.0 90.4 jit_solution(8907644328772847348)
XLA Ops:
  0.0 89.0 %shard_map.82 = f32[2,128]{1,0:T(2,128)} custom-call(bf16[2,96,256]{2,1,0:T(8,128)(2,1)} %acts.1, bf16[2,96,448]{2,1,0:T(8,128)(2,1)} %grads.1, s32[2]{0:T(128)} %counts.1, bf16[8192,256]{1,0:T(8,128)(2,1)} %basis_in.1, bf16[448,1792]{1,0:T(8,128)(2,1)} %bitcast.1, bf16[448,8192]{1,0:T(8,128)(2,1)} %eigvals.1, bf16[1,16,448]{2,1,0:T(8,128)(2,1)} %query_out.1, ...), custom_call_target="tpu_custom_call" | custom-call | tf_op jit(solution)/shard_map/pallas_call | solution.py:676
  89.0 0.8 reshape.3
  89.7 0.7 reduce_sum.9

commit v7 on v6

--- a/solution.py
+++ b/solution.py
@@ -653,12 +653,17 @@
         place, tiles2, landed2, sum2_send, sum2_recv
     )
     end_first()
+    for gather in (gather_acts, *gather_grads[:2]):
+        gather.finish()
+    for copy in qin_sent + qout_sent + sum1_sent:
+        copy.wait_send()
     end_second()
+    for gather in (*gather_grads[2:], gather_wide):
+        gather.finish()
+    for copy in z_sent:
+        copy.wait_send()
     out[...] = end_last()[:2]
-
-    for gather in (gather_acts, *gather_grads, gather_wide):
-        gather.finish()
-    for copy in qin_sent + qout_sent + z_sent + sum1_sent + sum2_sent:
+    for copy in sum2_sent:
         copy.wait_send()
 
 

time: 90.5 us -> 90.1 us (level)
  no operation moved by 1% of the time
where the time goes in v7:
time: 90.1 us; the launch traced here: 90 us
  Pallas kernels  88.6 us (98%)
    pallas_call x1, Pallas kernels, per_device(): pl.pallas_call(kernel, out_shape=jax.ShapeDtypeStruct((2, 128), F32), in_...  88.6 us

profile of v7, /device:TPU:1, one launch (start us, length us, event | category | flops | bytes accessed | tf_op | source)
XLA Modules:
  0.0 90.0 jit_solution(6899693097504538535)
XLA Ops:
  0.0 88.6 %shard_map.82 = f32[2,128]{1,0:T(2,128)} custom-call(bf16[2,96,256]{2,1,0:T(8,128)(2,1)} %acts.1, bf16[2,96,448]{2,1,0:T(8,128)(2,1)} %grads.1, s32[2]{0:T(128)} %counts.1, bf16[8192,256]{1,0:T(8,128)(2,1)} %basis_in.1, bf16[448,1792]{1,0:T(8,128)(2,1)} %bitcast.1, bf16[448,8192]{1,0:T(8,128)(2,1)} %eigvals.1, bf16[1,16,448]{2,1,0:T(8,128)(2,1)} %query_out.1, ...), custom_call_target="tpu_custom_call" | custom-call | tf_op jit(solution)/shard_map/pallas_call | solution.py:681
  88.6 0.8 reshape.3
  89.4 0.7 reduce_sum.9
